TPU v7x, 128 devices: a whole 4x4x4 slice. The times are simulated.
128 devices in a mesh: outer: 8 (over y, core), inner: 16 (over x, z).
Axes of the slice: x: 4, y: 4, z: 4, core: 2. Of those that a mesh axis runs over, the one named last changes fastest.
Arguments:
- points: float32 [262144, 64], P(('outer', 'inner')), may hold values from -2.5 to 2.5
- charges: float32 [262144, 128], P(('outer', 'inner')), may hold values from -0.4 to 0.4
- interp: float32 [262144, 256], P(('outer', 'inner')), may hold values from -0.25 to 0.25
- order: int32 [262144], P(('outer', 'inner')), may hold values from 0 to 262143, as said below
- near: int32 [512, 8], replicated, may hold values from 0 to 511, as said below
- far: int32 [512, 8], replicated, may hold values from 0 to 511, as said below
- skel: int32 [512, 256], P(('outer', 'inner')), may hold values from 0 to 511, as said below
Outputs:
- potential: float32 [262144, 128], P(('outer', 'inner'))
Inputs may be any that keep to these rules, and one draw needn't show every extreme that they name: `order`: A permutation; tree position p lies on device p // 2048 in the rows' layout, and each device's rows hold exactly 16 positions of every device. `near`: row g names leaf g first, then 8 - 1 distinct leaves on other devices with the same outer index (leaf h lies on device h // 4); the entries of one device's leaves name at most 2 leaves on any one other device, counting repeats, and some pair of devices reaches 2. `far`: row g names 8 distinct leaves on devices with the same inner index as leaf g and another outer index. `skel`: each row holds distinct values.
All inputs are finite; a program needn't handle non-finite values.
Results may differ from a plain program's by a relative error of at most 0.000082.
Values sent between devices are 32-bit elements; how exact they have to be, the bound alone decides.
A program may use at most 128 MiB of HBM per device.

v0:
```python
import jax
import jax.numpy as jnp
from jax import lax
from jax.sharding import PartitionSpec as P


def split_up(value, dim, peers):
    before, after = (value.shape[:dim], value.shape[dim + 1 :])
    return jnp.moveaxis(value.reshape(*before, peers, -1, *after), dim, 0)


def in_order(parts, dim):
    parts = jnp.moveaxis(parts, 0, dim)
    lengths = parts.shape
    return parts.reshape(*lengths[:dim], lengths[dim] * lengths[dim + 1], *lengths[dim + 2 :])


def joined_exchange(value, axis, axes, splits, concats):
    sizes = [lax.axis_size(a) for a in axes]
    parts = split_up(value, splits[0], sizes[0])
    parts = jnp.moveaxis(split_up(parts, splits[1] + 1, sizes[1]), 0, 1)
    inside = parts.shape[2:]
    parts = parts.reshape(-1, *inside)
    parts = lax.all_to_all(parts, axis, split_axis=0, concat_axis=0, tiled=True)
    parts = in_order(parts.reshape(*sizes, *inside), concats[0] + 1)
    return in_order(parts, concats[1])


def in_one_piece(arrays, axis, dim, along):
    ends, at = ([], 0)
    for a in arrays[:-1]:
        at += a.shape[along]
        ends.append(at)
    both = jnp.concatenate(arrays, axis=along)
    return tuple(jnp.split(lax.all_gather(both, axis, axis=dim, tiled=True), ends, axis=along))


def apply_tile(target, source, source_chg):
    cross = jnp.dot(
        target, source.T, precision=lax.Precision.HIGHEST, preferred_element_type=jnp.float32
    )
    dist_sq = (
        jnp.sum(target * target, axis=1)[:, None]
        + jnp.sum(source * source, axis=1)[None, :]
        - 2.0 * cross
    )
    kernel = jnp.exp(-dist_sq * (4.0 / target.shape[1]))
    return jnp.dot(
        kernel, source_chg, precision=lax.Precision.HIGHEST, preferred_element_type=jnp.float32
    )


def listed_sum(inputs):
    target, sources, source_chg = inputs
    return jnp.sum(
        jax.vmap(lambda source, charge: apply_tile(target, source, charge))(sources, source_chg),
        axis=0,
    )


def shards(points, charges, interp, order, near, far, skel):
    outer_count = lax.axis_size("outer")
    n_inner = lax.axis_size("inner")
    device_total = outer_count * n_inner
    row_count = points.shape[0]
    leaf_dev = skel.shape[0]
    leaf_size = row_count // leaf_dev
    per_device = row_count // device_total
    point_dim = points.shape[1]
    column_count = charges.shape[1]
    outer_idx = lax.axis_index("outer")
    inner_idx = lax.axis_index("inner")
    my_device = outer_idx * n_inner + inner_idx
    sorter = jnp.argsort(order)
    sent_pts = points[sorter]
    sent_chg = charges[sorter]
    slot_pos = (order[sorter] % row_count).astype(jnp.float32)
    sectioned = (
        joined_exchange(
            sent_pts.reshape(outer_count, n_inner, per_device, point_dim),
            ("outer", "inner"),
            ("outer", "inner"),
            (0, 1),
            (0, 1),
        ),
        joined_exchange(
            sent_chg.reshape(outer_count, n_inner, per_device, column_count),
            ("outer", "inner"),
            ("outer", "inner"),
            (0, 1),
            (0, 1),
        ),
        joined_exchange(
            slot_pos.reshape(outer_count, n_inner, per_device),
            ("outer", "inner"),
            ("outer", "inner"),
            (0, 1),
            (0, 1),
        ),
    )
    got_pts = sectioned[0].reshape(row_count, point_dim)
    got_chg = sectioned[1].reshape(row_count, column_count)
    got_pos = sectioned[2].reshape(row_count)
    positions = got_pos.astype(jnp.int32)
    placer = jnp.argsort(positions)
    leaf_pts = got_pts[placer].reshape(leaf_dev, leaf_size, point_dim)
    leaf_charge_block = got_chg[placer].reshape(leaf_dev, leaf_size, column_count)
    first_leaf = my_device * leaf_dev
    group_first = outer_idx * n_inner * leaf_dev
    near_rows = lax.dynamic_slice_in_dim(near, first_leaf, leaf_dev, 0)
    all_pts, all_chg = in_one_piece((leaf_pts, leaf_charge_block), "inner", 0, 2)
    picked = near_rows - group_first
    near_pts = all_pts[picked]
    near_chg = all_chg[picked]
    near_part = lax.map(listed_sum, (leaf_pts, near_pts, near_chg))
    leaf_interpolant = interp.reshape(leaf_dev, leaf_size, -1)
    skel_pts = jnp.take_along_axis(leaf_pts, skel[:, :, None], axis=1)
    skeleton_charge = jnp.einsum(
        "euq,eub->eqb", leaf_interpolant, leaf_charge_block, precision=lax.Precision.HIGHEST
    )
    column_pts, column_chg = in_one_piece((skel_pts, skeleton_charge), "outer", 0, 2)
    far_rows = lax.dynamic_slice_in_dim(far, first_leaf, leaf_dev, 0)
    far_column = far_rows // leaf_dev // n_inner * leaf_dev + far_rows % leaf_dev
    skeleton_potential = lax.map(
        listed_sum, (skel_pts, column_pts[far_column], column_chg[far_column])
    )
    far_field_part = jnp.einsum(
        "izx,ixb->izb", leaf_interpolant, skeleton_potential, precision=lax.Precision.HIGHEST
    )
    tree_pot = (near_part + far_field_part).reshape(row_count, column_count)
    outgoing = tree_pot[positions]
    returned = joined_exchange(
        outgoing.reshape(outer_count, n_inner, per_device, column_count),
        ("outer", "inner"),
        ("outer", "inner"),
        (0, 1),
        (0, 1),
    ).reshape(row_count, column_count)
    return returned[jnp.argsort(sorter)]


def solution(mesh):
    in_specs = (
        P(("outer", "inner"), None),
        P(("outer", "inner"), None),
        P(("outer", "inner"), None),
        P(("outer", "inner")),
        P(),
        P(),
        P(("outer", "inner"), None),
    )
    out_specs = P(("outer", "inner"), None)
    return jax.shard_map(shards, mesh=mesh, in_specs=in_specs, out_specs=out_specs, check_vma=False)
```

profile of v0, /device:TPU:1, one launch (start us, length us, event | category | flops | bytes accessed | tf_op | source)
XLA Modules:
  0.0 516.3 jit_solution(4453423770638041391)
XLA Ops:
  6.5 5.9 %sort.45 = (s32[2048]{0:T(1024)}, s32[2048]{0:T(1024)S(1)}) sort(s32[2048]{0:T(1024)} %param.14, s32[2048]{0:T(1024)S(1)} %iota.10), dimensions={0}, to_apply=%region_0.0 | sort | flops 22528 | bytes 32768 | tf_op jit(solution)/shard_map/jit(argsort)/sort | solution.py:74
  12.4 11.8 %gather_fusion.1 = s32[2048]{0:T(1024)S(1)} fusion(s32[2048]{0:T(1024)S(1)} %copy-done.1, s32[2048]{0:T(1024)S(1)} %fusion.67), kind=kCustom, calls=%fused_computation.1 | custom fusion | bytes 24576 | tf_op jit(solution)/shard_map/gather | solution.py:77
  25.1 11.5 %all-to-all-start.1 = ((f32[128,1,1,16]{3,2,1,0:T(1,128)}), f32[128,1,1,16]{3,2,1,0:T(1,128)S(1)}, u32[]{:S(2)}, u32[]{:S(2)}) async-start(f32[128,1,1,16]{3,2,1,0:T(1,128)} %copy.52), calls=%async_computation.1 | async-start | bytes 131072 | tf_op jit(solution)/shard_map/all_to_all | solution.py:24
  38.0 7.6 %gather_fusion = f32[2048,64]{1,0:T(8,128)} fusion(f32[2048,64]{1,0:T(8,128)S(1)} %copy.47, s32[2048]{0:T(1024)S(1)} %fusion.67), kind=kCustom, calls=%fused_computation | custom fusion | bytes 1056768 | tf_op jit(solution)/shard_map/gather | solution.py:75
  48.4 10.2 %all-to-all-start = ((f32[128,1,1024]{2,1,0:T(1,128)}), f32[128,1,1024]{2,1,0:T(1,128)}, u32[]{:S(2)}, u32[]{:S(2)}) async-start(f32[128,1,1024]{2,1,0:T(1,128)} %reshape.253), calls=%async_computation | async-start | bytes 1048576 | tf_op jit(solution)/shard_map/all_to_all | solution.py:24
  58.7 7.6 %gather_fusion.3 = f32[2048,128]{1,0:T(8,128)} fusion(f32[2048,128]{1,0:T(8,128)S(1)} %copy-done.2, s32[2048]{0:T(1024)S(1)} %fusion.67), kind=kCustom, calls=%fused_computation.3 | custom fusion | bytes 2105344 | tf_op jit(solution)/shard_map/gather | solution.py:76
  66.3 5.4 %all-to-all-done = f32[128,1,1024]{2,1,0:T(1,128)} async-done(((f32[128,1,1024]{2,1,0:T(1,128)}), f32[128,1,1024]{2,1,0:T(1,128)}, u32[]{:S(2)}, u32[]{:S(2)}) %all-to-all-start) | async-done | bytes 524320 | tf_op jit(solution)/shard_map/all_to_all | solution.py:24
  71.7 4.7 all-to-all-start.2
  76.7 5.0 sort.46
  82.2 3.7 reduce
  88.2 8.8 %gather_fusion.2 = f32[2048,64]{1,0:T(8,128)} fusion(f32[2048,64]{1,0:T(8,128)} %bitcast.192, s32[2048]{0:T(1024)S(1)} %fusion.68), kind=kCustom, calls=%fused_computation.2 | custom fusion | bytes 1056768 | tf_op jit(solution)/shard_map/gather | solution.py:106
  97.0 15.4 %gather_fusion.11 = f32[1024,64]{1,0:T(8,128)} fusion(f32[4,512,64]{2,1,0:T(8,128)} %bitcast.195, s32[1024]{0:T(1024)S(1)} %bitcast.193), kind=kCustom, calls=%fused_computation.11 | custom fusion | bytes 532480 | tf_op jit(solution)/shard_map/jit(take_along_axis)/gather | solution.py:117
  115.3 7.6 %gather_fusion.4 = f32[2048,128]{1,0:T(8,128)} fusion(f32[2048,128]{1,0:T(8,128)S(1)} %bitcast.189, s32[2048]{0:T(1024)S(1)} %fusion.68), kind=kCustom, calls=%fused_computation.4 | custom fusion | bytes 2105344 | tf_op jit(solution)/shard_map/gather | solution.py:107
  123.0 3.2 convolution_bitcast_fusion.1
  133.9 36.4 %all-gather.5.cloned.1.call-done = f32[32,256,192]{1,2,0:T(8,128)} async-done(((f32[4,256,192]{1,2,0:T(8,128)}), f32[32,256,192]{1,2,0:T(8,128)}) %all-gather.5.cloned.1.call-update) | async-done | bytes 6291472 | tf_op jit(solution)/shard_map/all_gather | solution.py:35
  170.3 3.1 split.18
  173.4 3.6 gather_fusion.7
  177.0 4.6 split.19
  181.7 5.6 %gather_fusion.8 = f32[32,256,128]{1,2,0:T(8,128)} fusion(f32[32,256,128]{1,2,0:T(8,128)} %split.19, s32[1024]{0:T(1024)S(1)} %pad_clamp_fusion), kind=kCustom, calls=%fused_computation.8 | custom fusion | bytes 8388736 | tf_op jit(solution)/shard_map/gather | solution.py:125
  187.3 29.7 %while.21 = (s32[]{:T(128)}, f32[4,256,128]{2,1,0:T(8,128)S(1)}, f32[4,256,64]{1,2,0:T(8,128)S(1)}, f32[4,8,256,64]{2,3,1,0:T(8,128)}, f32[4,8,256,128]{2,3,1,0:T(8,128)}, /*index=5*/s32[]{:T(128)}) while((s32[]{:T(128)}, f32[4,256,128]{2,1,0:T(8,128)S(1)}, f32[4,256,64]{1,2,0:T(8,128)S(1)}, f32[4,8,256,64]{2,3,1,0:T(8,128)}, ...), condition=%wide.region_9.10_spmd, body=%wide.region_6.9_spmd.sunk | while | flops 1210873600 | bytes 6574165 | solution.py:124
  187.3 2.9 fusion.109
  191.3 3.4 fusion.112
  194.7 2.9 fusion.109
  198.8 3.4 fusion.112
  202.2 2.9 fusion.109
  206.3 3.4 fusion.112
  209.6 2.9 fusion.109
  213.7 3.4 fusion.112
  217.1 109.4 %all-gather.3.cloned.1.call-done = f32[64,512,192]{1,2,0:T(8,128)} async-done(((f32[4,512,192]{1,2,0:T(8,128)}), f32[64,512,192]{1,2,0:T(8,128)}) %all-gather.3.cloned.1.call-update) | async-done | bytes 25165840 | tf_op jit(solution)/shard_map/all_gather | solution.py:35
  326.5 8.4 %split.16 = f32[64,512,64]{1,2,0:T(8,128)} slice(f32[64,512,192]{1,2,0:T(8,128)} %all-gather.3.cloned.1.call-done), slice={[0:64], [0:512], [0:64]} | slice | bytes 16777216 | tf_op jit(solution)/shard_map/split | solution.py:35
  334.9 6.1 %gather_fusion.5 = f32[32,512,64]{1,2,0:T(8,128)} fusion(f32[64,512,64]{1,2,0:T(8,128)} %split.16, s32[1024]{0:T(1024)S(1)} %pad_clamp_fusion.1), kind=kCustom, calls=%fused_computation.5 | custom fusion | bytes 8388736 | tf_op jit(solution)/shard_map/gather | solution.py:113
  341.0 11.8 %split.17 = f32[64,512,128]{1,2,0:T(8,128)} slice(f32[64,512,192]{1,2,0:T(8,128)} %all-gather.3.cloned.1.call-done), slice={[0:64], [0:512], [64:192]} | slice | bytes 33554432 | tf_op jit(solution)/shard_map/split | solution.py:35
  352.8 10.1 %gather_fusion.6 = f32[32,512,128]{1,2,0:T(8,128)} fusion(f32[64,512,128]{1,2,0:T(8,128)} %split.17, s32[1024]{0:T(1024)S(1)} %pad_clamp_fusion.1), kind=kCustom, calls=%fused_computation.6 | custom fusion | bytes 16777344 | tf_op jit(solution)/shard_map/gather | solution.py:114
  362.9 98.4 %while.20 = (s32[]{:T(128)}, f32[4,512,128]{1,2,0:T(8,128)}, f32[4,512,64]{1,2,0:T(8,128)S(1)}, f32[4,8,512,64]{2,3,1,0:T(8,128)}, f32[4,8,512,128]{2,3,1,0:T(8,128)}, /*index=5*/s32[]{:T(128)}) while((s32[]{:T(128)}, f32[4,512,128]{1,2,0:T(8,128)}, f32[4,512,64]{1,2,0:T(8,128)S(1)}, f32[4,8,512,64]{2,3,1,0:T(8,128)}, ...), condition=%wide.region_5.6_spmd, body=%wide.region_2.5_spmd.sunk | while | flops 4842909184 | bytes 21534804 | solution.py:115
  373.3 8.1 %fusion.101 = f32[512,8,512]{2,0,1:T(8,128)S(1)} fusion(f32[4,8,512,64]{2,3,1,0:T(8,128)} %get-tuple-element.196, s32[]{:T(128)S(6)} %copy.81, f32[4,512,64]{1,2,0:T(8,128)S(1)} %get-tuple-element.195), kind=kOutput, calls=%fused_computation.27.clone.1 | convolution fusion | flops 1610612736 | bytes 9569280 | tf_op jit(solution)/shard_map/while/body/eval_jaxpr/vmap()/dot_general | solution.py:39
  382.8 12.5 %fusion.104 = f32[4,512,128]{1,2,0:T(8,128)} fusion(f32[4,512,128]{1,2,0:T(8,128)} %get-tuple-element.188, s32[]{:T(128)S(6)} %copy.81, f32[4,8,512,128]{2,3,1,0:T(8,128)} %get-tuple-element.197, f32[512,8,512]{2,0,1:T(8,128)S(1)} %fusion.101, f32[8,512]{1,0:T(8,128)S(1)} %fusion.102, f32[512]{0:T(512)S(1)} %fusion.103), kind=kOutput, calls=%fused_computation.26.clone.1 | convolution fusion | flops 3231711232 | bytes 10767360 | tf_op jit(solution)/shard_map/while/body/eval_jaxpr/vmap()/dot_general | solution.py:48
  395.3 8.1 %fusion.101 = f32[512,8,512]{2,0,1:T(8,128)S(1)} fusion(f32[4,8,512,64]{2,3,1,0:T(8,128)} %get-tuple-element.196, s32[]{:T(128)S(6)} %copy.81, f32[4,512,64]{1,2,0:T(8,128)S(1)} %get-tuple-element.195), kind=kOutput, calls=%fused_computation.27.clone.1 | convolution fusion | flops 1610612736 | bytes 9569280 | tf_op jit(solution)/shard_map/while/body/eval_jaxpr/vmap()/dot_general | solution.py:39
  404.8 12.5 %fusion.104 = f32[4,512,128]{1,2,0:T(8,128)} fusion(f32[4,512,128]{1,2,0:T(8,128)} %get-tuple-element.188, s32[]{:T(128)S(6)} %copy.81, f32[4,8,512,128]{2,3,1,0:T(8,128)} %get-tuple-element.197, f32[512,8,512]{2,0,1:T(8,128)S(1)} %fusion.101, f32[8,512]{1,0:T(8,128)S(1)} %fusion.102, f32[512]{0:T(512)S(1)} %fusion.103), kind=kOutput, calls=%fused_computation.26.clone.1 | convolution fusion | flops 3231711232 | bytes 10767360 | tf_op jit(solution)/shard_map/while/body/eval_jaxpr/vmap()/dot_general | solution.py:48
  417.3 8.1 %fusion.101 = f32[512,8,512]{2,0,1:T(8,128)S(1)} fusion(f32[4,8,512,64]{2,3,1,0:T(8,128)} %get-tuple-element.196, s32[]{:T(128)S(6)} %copy.81, f32[4,512,64]{1,2,0:T(8,128)S(1)} %get-tuple-element.195), kind=kOutput, calls=%fused_computation.27.clone.1 | convolution fusion | flops 1610612736 | bytes 9569280 | tf_op jit(solution)/shard_map/while/body/eval_jaxpr/vmap()/dot_general | solution.py:39
  426.8 12.5 %fusion.104 = f32[4,512,128]{1,2,0:T(8,128)} fusion(f32[4,512,128]{1,2,0:T(8,128)} %get-tuple-element.188, s32[]{:T(128)S(6)} %copy.81, f32[4,8,512,128]{2,3,1,0:T(8,128)} %get-tuple-element.197, f32[512,8,512]{2,0,1:T(8,128)S(1)} %fusion.101, f32[8,512]{1,0:T(8,128)S(1)} %fusion.102, f32[512]{0:T(512)S(1)} %fusion.103), kind=kOutput, calls=%fused_computation.26.clone.1 | convolution fusion | flops 3231711232 | bytes 10767360 | tf_op jit(solution)/shard_map/while/body/eval_jaxpr/vmap()/dot_general | solution.py:48
  439.3 8.1 %fusion.101 = f32[512,8,512]{2,0,1:T(8,128)S(1)} fusion(f32[4,8,512,64]{2,3,1,0:T(8,128)} %get-tuple-element.196, s32[]{:T(128)S(6)} %copy.81, f32[4,512,64]{1,2,0:T(8,128)S(1)} %get-tuple-element.195), kind=kOutput, calls=%fused_computation.27.clone.1 | convolution fusion | flops 1610612736 | bytes 9569280 | tf_op jit(solution)/shard_map/while/body/eval_jaxpr/vmap()/dot_general | solution.py:39
  448.8 12.5 %fusion.104 = f32[4,512,128]{1,2,0:T(8,128)} fusion(f32[4,512,128]{1,2,0:T(8,128)} %get-tuple-element.188, s32[]{:T(128)S(6)} %copy.81, f32[4,8,512,128]{2,3,1,0:T(8,128)} %get-tuple-element.197, f32[512,8,512]{2,0,1:T(8,128)S(1)} %fusion.101, f32[8,512]{1,0:T(8,128)S(1)} %fusion.102, f32[512]{0:T(512)S(1)} %fusion.103), kind=kOutput, calls=%fused_computation.26.clone.1 | convolution fusion | flops 3231711232 | bytes 10767360 | tf_op jit(solution)/shard_map/while/body/eval_jaxpr/vmap()/dot_general | solution.py:48
  461.3 4.5 fusion.64
  467.4 7.6 %gather_fusion.9 = f32[2048,128]{1,0:T(8,128)} fusion(f32[2048,128]{1,0:T(8,128)S(1)} %bitcast.191, s32[2048]{0:T(1024)S(1)} %broadcast_clamp_fusion), kind=kCustom, calls=%fused_computation.9 | custom fusion | bytes 2105344 | tf_op jit(solution)/shard_map/gather | solution.py:131
  475.1 7.9 %all-to-all-start.3 = ((f32[128,1,1,16,128]{4,3,2,1,0:T(8,128)}), f32[128,1,1,16,128]{4,3,2,1,0:T(8,128)S(1)}, u32[]{:S(2)}, u32[]{:S(2)}) async-start(f32[128,1,1,16,128]{4,3,2,1,0:T(8,128)} %bitcast.202), calls=%async_computation.3 | async-start | bytes 2097152 | tf_op jit(solution)/shard_map/all_to_all | solution.py:24
  483.0 5.0 sort.47
  488.0 13.6 %all-to-all-done.3 = f32[128,1,1,16,128]{4,3,2,1,0:T(8,128)S(1)} async-done(((f32[128,1,1,16,128]{4,3,2,1,0:T(8,128)}), f32[128,1,1,16,128]{4,3,2,1,0:T(8,128)S(1)}, u32[]{:S(2)}, u32[]{:S(2)}) %all-to-all-start.3) | async-done | bytes 1048608 | tf_op jit(solution)/shard_map/all_to_all | solution.py:24
  501.6 7.6 %gather_fusion.10 = f32[2048,128]{1,0:T(8,128)} fusion(f32[2048,128]{1,0:T(8,128)S(1)} %bitcast.190, s32[2048]{0:T(1024)S(1)} %fusion.69), kind=kCustom, calls=%fused_computation.10 | custom fusion | bytes 2105344 | tf_op jit(solution)/shard_map/gather | solution.py:139
  (72 shorter events, 30.4 us)
Async XLA Ops:
  6.5 116.4 %copy-start = (f32[2048,256]{1,0:T(8,128)S(1)}, f32[2048,256]{1,0:T(8,128)}, u32[]{:S(2)}) copy-start(f32[2048,256]{1,0:T(8,128)} %param.13) | copy-start | bytes 6291460
  6.5 5.9 %copy-start.1 = (s32[2048]{0:T(1024)S(1)}, s32[2048]{0:T(1024)}, u32[]{:S(2)}) copy-start(s32[2048]{0:T(1024)} %param.14) | copy-start | bytes 24580
  25.1 23.3 %all-to-all-start.1 = ((f32[128,1,1,16]{3,2,1,0:T(1,128)}), f32[128,1,1,16]{3,2,1,0:T(1,128)S(1)}, u32[]{:S(2)}, u32[]{:S(2)}) async-start(f32[128,1,1,16]{3,2,1,0:T(1,128)} %copy.52), calls=%async_computation.1 | async-start | bytes 131072 | tf_op jit(solution)/shard_map/all_to_all | solution.py:24
  45.7 13.0 %copy-start.2 = (f32[2048,128]{1,0:T(8,128)S(1)}, f32[2048,128]{1,0:T(8,128)}, u32[]{:S(2)}) copy-start(f32[2048,128]{1,0:T(8,128)} %param.12) | copy-start | bytes 3145732
  48.4 23.3 %all-to-all-start = ((f32[128,1,1024]{2,1,0:T(1,128)}), f32[128,1,1024]{2,1,0:T(1,128)}, u32[]{:S(2)}, u32[]{:S(2)}) async-start(f32[128,1,1024]{2,1,0:T(1,128)} %reshape.253), calls=%async_computation | async-start | bytes 1048576 | tf_op jit(solution)/shard_map/all_to_all | solution.py:24
  58.7 17.8 %copy-start.5 = (s32[4,256]{1,0:T(4,128)S(1)}, s32[4,256]{1,0:T(4,128)}, u32[]{:S(2)}) copy-start(s32[4,256]{1,0:T(4,128)} %param.17) | copy-start | bytes 12292
  71.7 43.6 %all-to-all-start.2 = ((f32[128,1,1,16,128]{4,3,2,1,0:T(8,128)}), f32[128,1,1,16,128]{4,3,2,1,0:T(8,128)S(1)}, u32[]{:S(2)}, u32[]{:S(2)}) async-start(f32[128,1,1,16,128]{4,3,2,1,0:T(8,128)} %bitcast.201), calls=%async_computation.2 | async-start | bytes 2097152 | tf_op jit(solution)/shard_map/all_to_all | solution.py:24
  76.4 93.9 %all-gather.5.cloned.1.call-start = ((), (), s32[]{:S(2)}) async-start(), calls=%async_computation.5 | async-start | bytes 7077888 | tf_op jit(solution)/shard_map/all_gather | solution.py:35
  123.0 4.6 copy-start.3
  127.1 199.3 %all-gather.3.cloned.1.call-start = ((), (), s32[]{:S(2)}) async-start(), calls=%async_computation.4 | async-start | bytes 26738688 | tf_op jit(solution)/shard_map/all_gather | solution.py:35
  352.8 10.1 %copy-start.4 = (f32[4,512,64]{1,2,0:T(8,128)S(1)}, f32[4,512,64]{1,2,0:T(8,128)}, u32[]{:S(2)}) copy-start(f32[4,512,64]{1,2,0:T(8,128)} %copy.57) | copy-start | bytes 1572868
  475.1 26.5 %all-to-all-start.3 = ((f32[128,1,1,16,128]{4,3,2,1,0:T(8,128)}), f32[128,1,1,16,128]{4,3,2,1,0:T(8,128)S(1)}, u32[]{:S(2)}, u32[]{:S(2)}) async-start(f32[128,1,1,16,128]{4,3,2,1,0:T(8,128)} %bitcast.202), calls=%async_computation.3 | async-start | bytes 2097152 | tf_op jit(solution)/shard_map/all_to_all | solution.py:24
Sparse Core Ops, SparseCore 0:
  127.3 42.9 all-gather.4
  172.5 153.9 all-gather.2
where the time goes:
time: 526 us; the launch traced here: 516 us
  waiting for transfers between devices  165 us (31%)
  local copies, waits for them, and re-layouts  142 us (27%)
  matrix products  115 us (22%)
  other arithmetic  35.1 us (7%)
  starting transfers between devices  34.8 us (7%)
  between operations  13.9 us (3%)
  loops' own time  10.6 us (2%)
    all_gather x2, waiting for transfers between devices, in_one_piece(): lax.all_gather(both, axis, axis=dim, tiled=True)  146 us
    dot_general x8, matrix products, apply_tile(): jnp.dot(kernel, source_chg, precision=lax.Precision.HIGHEST, preferred_el...  63.5 us
    dot_general x8, matrix products, apply_tile(): jnp.dot(target, source.T, precision=lax.Precision.HIGHEST, preferred_elem...  43.9 us
    all_to_all x4, starting transfers between devices, joined_exchange(): parts = lax.all_to_all(parts, axis, split_axis=0, concat_axis=0, tiled=True)  34.3 us
    split x4, local copies, waits for them, and re-layouts, in_one_piece(): jnp.split(lax.all_gather(both, axis, axis=dim, tiled=True), ends, axis=al...  28 us
    all_to_all x4, waiting for transfers between devices, joined_exchange(): parts = lax.all_to_all(parts, axis, split_axis=0, concat_axis=0, tiled=True)  19 us
    gather x2, local copies, waits for them, and re-layouts, shards(): skel_pts = jnp.take_along_axis(leaf_pts, skel[:, :, None], axis=1)  17.3 us
    gather x3, local copies, waits for them, and re-layouts, shards(): slot_pos = (order[sorter] % row_count).astype(jnp.float32)  11.9 us
  transfers between devices with their start and end apart: 6, of which 4 were waited for; matrix products, arithmetic and copies ran while one was open for 22% of the time, Pallas kernels for 0%

commit v1 on v0

v1 whole, which is shorter than its diff:
```python
import functools
import math

import jax
import jax.numpy as jnp
from jax import lax
from jax.experimental import pallas as pl
from jax.experimental.pallas import tpu as pltpu
from jax.sharding import PartitionSpec as P

F32, BF16, I32 = jnp.float32, jnp.bfloat16, jnp.int32
MESH = pl.DeviceIdType.MESH
VMEM_LIMIT = 60 * 1024 * 1024

ROWS = 2048
DEVS = 128
LEAF = 512
HALF = 256
DIM = 64
RHS = 128
BLK = HALF + 128
SCALE = math.log2(math.e) * 4.0 / DIM


def vspec():
    return pl.BlockSpec(memory_space=pltpu.VMEM)


def sspec():
    return pl.BlockSpec(memory_space=pltpu.SMEM)


def dot(a, b, contract=((1,), (0,))):
    return lax.dot_general(a, b, (contract, ((), ())), preferred_element_type=F32)


def hi_lo(v):
    hi = v.astype(BF16)
    return hi, (v - hi.astype(F32)).astype(BF16)


def dot3(a, b, contract=((1,), (0,))):
    ah, al = hi_lo(a)
    bh, bl = hi_lo(b)
    return dot(ah, bh, contract) + dot(ah, bl, contract) + dot(al, bh, contract)


def three(v):
    hi = v.astype(BF16).astype(F32)
    rest = v - hi
    mid = rest.astype(BF16).astype(F32)
    return hi, mid, rest - mid


def rank_kernel(order_ref, rank_ref):
    sub = lax.broadcasted_iota(I32, (128, 128), 0)
    lane = lax.broadcasted_iota(I32, (128, 128), 1)
    before = (sub < lane).astype(F32).astype(BF16)
    ones = jnp.ones((128, 128), BF16)
    base = jnp.zeros((128, 128), F32)
    for r in range(ROWS // 128):
        owner = order_ref[r : r + 1, :] // ROWS
        hit = (sub == owner).astype(F32)
        hit16 = hit.astype(BF16)
        seen = dot(hit16, before) + base
        base = base + dot(hit16, ones)
        count = jnp.sum(hit * seen, axis=0, keepdims=True)
        rank_ref[r : r + 1, :] = owner * 16 + count.astype(I32)


def rank_rows(order):
    return pl.pallas_call(
        rank_kernel,
        out_shape=jax.ShapeDtypeStruct((ROWS // 128, 128), I32),
        in_specs=[vspec()],
        out_specs=vspec(),
    )(order.reshape(ROWS // 128, 128))


def send_kernel(rank_ref, order_ref, pts_ref, chg_ref, sent_ref, wide):
    lane = lax.broadcasted_iota(I32, (128, 128), 1)
    for r in range(ROWS // 128):
        rows = pl.ds(r * 128, 128)
        wide[rows, 0:DIM] = pts_ref[rows, :]
        pos = (order_ref[r : r + 1, :] % ROWS).astype(F32)
        column = jnp.transpose(jnp.broadcast_to(pos, (128, 128)))
        wide[rows, DIM:128] = column[:, 0:DIM]

    def body(b, carry):
        for u in range(16):
            n = b * 16 + u
            to = rank_ref[n]
            dev, row = to // 16, to % 16
            sent_ref[dev, pl.ds(row, 1), :] = chg_ref[pl.ds(n, 1), :]
            sent_ref[dev, pl.ds(row + 16, 1), :] = wide[pl.ds(n, 1), :]
        return carry

    lax.fori_loop(0, ROWS // 16, body, 0)


def pack_rows(rank, order, points, charges):
    return pl.pallas_call(
        send_kernel,
        out_shape=jax.ShapeDtypeStruct((DEVS, 32, 128), F32),
        in_specs=[sspec(), vspec(), vspec(), vspec()],
        out_specs=vspec(),
        scratch_shapes=[pltpu.VMEM((ROWS, 128), F32)],
        compiler_params=pltpu.CompilerParams(vmem_limit_bytes=VMEM_LIMIT),
    )(rank, order.reshape(ROWS // 128, 128), points, charges)


def target_operand(x):
    n = x.shape[0]
    hi, lo = hi_lo(x * (2.0 * SCALE))
    norm = jnp.sum(x * x, axis=1, keepdims=True) * (-SCALE)
    n0, n1, n2 = three(norm)
    lane = lax.broadcasted_iota(I32, (n, DIM), 1)
    tail = jnp.where(
        lane == 0, n0, jnp.where(lane == 1, n1, jnp.where(lane == 2, n2, jnp.where(lane < 6, 1.0, 0.0)))
    )
    return jnp.concatenate([hi, hi, lo, tail.astype(BF16)], axis=1)


def place_kernel(pos_ref, skel_ref, got_ref, interp_ref, blk_ref, fblk_ref, tgt_ref, stgt_ref, pts, chg, sk):
    def place(b, carry):
        for u in range(16):
            at = pos_ref[b * 16 + u]
            chg[pl.ds(at, 1), :] = got_ref[b, u : u + 1, :]
            pts[pl.ds(at, 1), :] = got_ref[b, 16 + u : 17 + u, :]
        return carry

    lax.fori_loop(0, DEVS, place, 0)

    def leaf(g, carry):
        def pick(b, inner):
            for u in range(16):
                q = b * 16 + u
                sk[pl.ds(q, 1), :] = pts[pl.ds(g * LEAF + skel_ref[g, q], 1), :]
            return inner

        lax.fori_loop(0, 16, pick, 0)
        for h in range(2):
            rows = pl.ds(pl.multiple_of(g * LEAF + h * HALF, HALF), HALF)
            blk_ref[h, g, 0:HALF, :] = chg[rows, :]
            x = pts[rows, :]
            xt = jnp.transpose(x)
            blk_ref[h, g, HALF : HALF + 64, :] = xt[0:64, 0:128]
            blk_ref[h, g, HALF + 64 : BLK, :] = xt[0:64, 128:256]
            tgt_ref[g, h * HALF : (h + 1) * HALF, :] = target_operand(x[:, 0:DIM])
        s = sk[...]
        st = jnp.transpose(s)
        fblk_ref[g, HALF : HALF + 64, :] = st[0:64, 0:128]
        fblk_ref[g, HALF + 64 : BLK, :] = st[0:64, 128:256]
        stgt_ref[g] = target_operand(s[:, 0:DIM])
        rows = pl.ds(pl.multiple_of(g * LEAF, LEAF), LEAF)
        fblk_ref[g, 0:HALF, :] = dot3(interp_ref[rows, :], chg[rows, :], ((0,), (0,)))
        return carry

    lax.fori_loop(0, 4, leaf, 0)


def place_rows(pos, skel, got, interp):
    return pl.pallas_call(
        place_kernel,
        out_shape=[
            jax.ShapeDtypeStruct((2, 4, BLK, 128), F32),
            jax.ShapeDtypeStruct((4, BLK, 128), F32),
            jax.ShapeDtypeStruct((4, LEAF, 256), BF16),
            jax.ShapeDtypeStruct((4, HALF, 256), BF16),
        ],
        in_specs=[sspec(), sspec(), vspec(), vspec()],
        out_specs=[vspec()] * 4,
        scratch_shapes=[
            pltpu.VMEM((ROWS, 128), F32),
            pltpu.VMEM((ROWS, 128), F32),
            pltpu.VMEM((HALF, 128), F32),
        ],
        compiler_params=pltpu.CompilerParams(vmem_limit_bytes=VMEM_LIMIT),
    )(pos, skel, got, interp)


def source_operand(block, scale):
    xt = jnp.concatenate([block[HALF : HALF + 64, :], block[HALF + 64 : BLK, :]], axis=1)
    hi, lo = hi_lo(xt)
    norm = jnp.sum(xt * xt, axis=0, keepdims=True) * (-SCALE)
    n0, n1, n2 = three(norm)
    row = lax.broadcasted_iota(I32, (16, HALF), 0)
    tail = jnp.where(
        row < 3, 1.0, jnp.where(row == 3, n0, jnp.where(row == 4, n1, jnp.where(row == 5, n2, 0.0)))
    )
    right = jnp.concatenate([hi, lo, hi, tail.astype(BF16), jnp.zeros((48, HALF), BF16)], axis=0)
    chg = block[0:HALF, :]
    if scale is not None:
        chg = chg * scale
    ch, cl = hi_lo(chg)
    return right, jnp.concatenate([ch, cl], axis=1), ch


def tile(target, operand):
    right, both, ch = operand
    g = jnp.exp2(dot(target, right))
    gh, gl = hi_lo(g)
    wide = dot(gh, both)
    return wide[:, 0:128] + wide[:, 128:256] + dot(gl, ch)


STEP = 128


def exchange_kernel(
    code, near_at, far_at, blk, fblk, tgt, stgt, interp, pot,
    p1a1, p1a2, p1a3, p1b1, p1b2, p1b3, sb, p2, p3, fb, ob,
    s1, r1, s2, r2, s3, r3, sf, rf,
):
    o, i = lax.axis_index("outer"), lax.axis_index("inner")
    y, c, x, z = o // 2, o % 2, i // 4, i % 4
    p1 = ((None, p1a1, p1a2, p1a3), (None, p1b1, p1b2, p1b3))

    def at_inner(dx, dz):
        return ((x + dx + 4) % 4) * 4 + (z + dz + 4) % 4

    def off(h, d1, d2):
        return at_inner(d1, d2) if h == 0 else at_inner(d2, d1)

    def first(h, d):
        return (o, off(h, d, 0))

    def second(h, d):
        return (o, off(h, 0, d))

    def along_y(d):
        return (((y + d + 4) % 4) * 2 + c, i)

    sibling = (y * 2 + 1 - c, i)

    barrier = pltpu.get_barrier_semaphore()
    peers = [first(0, 1), first(0, -1), second(0, 1), second(0, -1), along_y(1), along_y(-1), sibling]
    for peer in peers:
        pl.semaphore_signal(barrier, inc=1, device_id=peer, device_id_type=MESH)
    pl.semaphore_wait(barrier, len(peers))

    def copy(src, dst, send, recv, to):
        return pltpu.make_async_remote_copy(
            src_ref=src, dst_ref=dst, send_sem=send, recv_sem=recv, device_id=to, device_id_type=MESH
        )

    def own_first(h, k):
        return copy(blk.at[h], p1[h][1 if k == 0 else 3], s1.at[h, k], r1.at[h, k], first(h, 1 if k == 0 else -1))

    def onward(h, k):
        part = pl.ds(2 * k, 2)
        src = p1[h][1 if k == 0 else 3].at[part]
        return copy(src, p1[h][2].at[part], s1.at[h, 2 + k], r1.at[h, 2 + k], first(h, 1 if k == 0 else -1))

    def slots(h, d, k):
        return copy(sb.at[h, d, k], p2.at[h, d, k], s2.at[h, d, k], r2.at[h, d, k], second(h, 1 if k == 0 else -1))

    def relay(h, d, k):
        return copy(p2.at[h, d, k, 2], p3.at[h, d, k], s3.at[h, d, k], r3.at[h, d, k], second(h, 1 if k == 0 else -1))

    def fbuf(dy, dc, lo=0, n=4):
        return fb.at[pl.ds((dy * 2 + dc - 1) * 4 + lo, n)]

    far_copies = {
        "up": copy(fblk, fbuf(1, 0), sf.at[0], rf.at[0], along_y(1)),
        "down": copy(fblk, fbuf(3, 0), sf.at[1], rf.at[1], along_y(-1)),
        "own": copy(fblk, fbuf(0, 1), sf.at[2], rf.at[2], sibling),
        "up2": copy(fbuf(1, 0, 0, 2), fbuf(2, 0, 0, 2), sf.at[3], rf.at[3], along_y(1)),
        "down2": copy(fbuf(3, 0, 2, 2), fbuf(2, 0, 2, 2), sf.at[4], rf.at[4], along_y(-1)),
        "side1": copy(fbuf(1, 0), fbuf(1, 1), sf.at[5], rf.at[5], sibling),
        "side3": copy(fbuf(3, 0), fbuf(3, 1), sf.at[6], rf.at[6], sibling),
        "side2": copy(fbuf(2, 0), fbuf(2, 1), sf.at[7], rf.at[7], sibling),
    }

    def leaf_code(dest, src, j):
        return code[(dest * 16 + src) * 2 + j]

    def fill(h, d):
        src = off(h, -d, 0)
        for k in range(2):
            for slot in range(3):
                dest = off(h, 0, (1 if k == 0 else -1) if slot < 2 else 2)
                leaf = leaf_code(dest, src, slot if slot < 2 else k) % 4
                if d == 0:
                    sb[h, d, k, slot] = blk[h, leaf]
                else:
                    sb[h, d, k, slot] = p1[h][d][leaf]
            slots(h, d, k).start()

    def add_tile(block, g, scale, at, n=LEAF):
        operand = source_operand(block, scale)
        for r in range(0, n, STEP):
            rows = pl.ds(r, STEP)
            ob[at, rows, :] += tile(tgt[g, rows, :], operand)

    def slot_tiles(h, d, e, which):
        dx, dz = (d, e) if h == 0 else (e, d)
        src = at_inner(-dx, -dz)
        for j, load in which:
            v = leaf_code(i, src, j)
            add_tile(load(v % 4), (v // 4) % 4, (v // 16).astype(F32), (dx * 4 + dz) * 2 + j)

    own_first(0, 0).start()
    own_first(0, 1).start()
    own_first(1, 0).start()
    own_first(1, 1).start()
    far_copies["up"].start()
    far_copies["down"].start()
    far_copies["own"].start()
    fill(0, 0)
    fill(1, 0)

    def zero(t, carry):
        ob[t] = jnp.zeros((LEAF, 128), F32)
        return carry

    lax.fori_loop(0, 32, zero, 0)

    def own(t, carry):
        g, h = t // 2, t % 2
        add_tile(blk[h, g], g, None, 0)
        rows = pl.ds(pl.multiple_of(g * LEAF, LEAF), LEAF)

        @pl.when(h == 1)
        def _():
            pot[rows, :] = ob[0]
            ob[0] = jnp.zeros((LEAF, 128), F32)

        return carry

    lax.fori_loop(0, 8, own, 0)

    for k in range(2):
        for h in range(2):
            own_first(h, k).wait_recv()
            onward(h, k).start()
            fill(h, 1 if k == 0 else 3)
    for name, more in (("up", ("up2", "side1")), ("down", ("down2", "side3")), ("own", ())):
        far_copies[name].wait_recv()
        for m in more:
            far_copies[m].start()

    def first_tiles(d):
        for h in range(2):
            slot_tiles(h, d, 0, [(j, lambda leaf, b=p1[h][d]: b[leaf]) for j in range(2)])

    first_tiles(1)
    far_copies["up2"].wait_recv()
    far_copies["down2"].wait_recv()
    far_copies["side2"].start()
    for h in range(2):
        onward(h, 0).wait_recv()
        onward(h, 1).wait_recv()
        fill(h, 2)
    first_tiles(3)

    def arrive(d):
        for h in range(2):
            for k in range(2):
                slots(h, d, k).wait_recv()
                relay(h, d, k).start()

    def second_tiles(d):
        for h in range(2):
            for k in range(2):
                slot_tiles(h, d, 1 if k == 0 else 3, [(j, lambda leaf, k=k, j=j: p2[h, d, k, j]) for j in range(2)])

    arrive(0)
    first_tiles(2)
    second_tiles(0)
    for name in ("side1", "side3", "side2"):
        far_copies[name].wait_recv()

    def far_leaf(g, carry):
        def one(k, q):
            operand = source_operand(fb[far_at[g * 8 + k]], None)
            return q + tile(stgt[g], operand)

        q = lax.fori_loop(0, 8, one, jnp.zeros((HALF, 128), F32))
        rows = pl.ds(pl.multiple_of(g * LEAF, LEAF), LEAF)
        pot[rows, :] += dot3(interp[rows, :], q)
        return carry

    lax.fori_loop(0, 4, far_leaf, 0)

    def relay_tiles(d):
        for h in range(2):
            for k in range(2):
                relay(h, d, k).wait_recv()
            slot_tiles(h, d, 2, [(j, lambda leaf, j=j: p3[h, d, j]) for j in range(2)])

    arrive(1)
    second_tiles(1)
    arrive(3)
    second_tiles(3)
    relay_tiles(0)
    arrive(2)
    second_tiles(2)
    relay_tiles(1)
    relay_tiles(3)
    relay_tiles(2)

    def finish(g, carry):
        rows = pl.ds(pl.multiple_of(g * LEAF, LEAF), LEAF)
        total = pot[rows, :]
        for k in range(7):
            total = total + ob[near_at[g * 7 + k]]
        pot[rows, :] = total
        return carry

    lax.fori_loop(0, 4, finish, 0)

    for h in range(2):
        for k in range(2):
            own_first(h, k).wait_send()
            onward(h, k).wait_send()
            for d in range(4):
                slots(h, d, k).wait_send()
                relay(h, d, k).wait_send()
    for one in far_copies.values():
        one.wait_send()


def exchange(code, near_at, far_at, blk, fblk, tgt, stgt, interp):
    dma = pltpu.SemaphoreType.DMA
    return pl.pallas_call(
        exchange_kernel,
        out_shape=jax.ShapeDtypeStruct((ROWS, RHS), F32),
        in_specs=[sspec()] * 3 + [vspec()] * 5,
        out_specs=vspec(),
        scratch_shapes=[pltpu.VMEM((4, BLK, 128), F32)] * 6
        + [
            pltpu.VMEM((2, 4, 2, 3, BLK, 128), F32),
            pltpu.VMEM((2, 4, 2, 3, BLK, 128), F32),
            pltpu.VMEM((2, 4, 2, BLK, 128), F32),
            pltpu.VMEM((28, BLK, 128), F32),
            pltpu.VMEM((32, LEAF, 128), F32),
            dma((2, 4)),
            dma((2, 4)),
            dma((2, 4, 2)),
            dma((2, 4, 2)),
            dma((2, 4, 2)),
            dma((2, 4, 2)),
            dma((8,)),
            dma((8,)),
        ],
        compiler_params=pltpu.CompilerParams(
            vmem_limit_bytes=VMEM_LIMIT, collective_id=0, has_side_effects=True
        ),
    )(code, near_at, far_at, blk, fblk, tgt, stgt, interp)


def gather_kernel(idx_ref, src_ref, dst_ref):
    def body(b, carry):
        for u in range(16):
            n = b * 16 + u
            dst_ref[pl.ds(n, 1), :] = src_ref[pl.ds(idx_ref[n], 1), :]
        return carry

    lax.fori_loop(0, ROWS // 16, body, 0)


def gather_rows(idx, src):
    return pl.pallas_call(
        gather_kernel,
        out_shape=jax.ShapeDtypeStruct((ROWS, RHS), F32),
        in_specs=[sspec(), vspec()],
        out_specs=vspec(),
        compiler_params=pltpu.CompilerParams(vmem_limit_bytes=VMEM_LIMIT),
    )(idx, src)


def tables(near, far):
    o, i = lax.axis_index("outer"), lax.axis_index("inner")
    y, c, x, z = o // 2, o % 2, i // 4, i % 4
    rows = lax.dynamic_slice_in_dim(near, o * 64, 64, 0)
    entry = rows[:, 1:].reshape(16, 28)
    src, leaf = (entry // 4) % 16, entry % 4
    target = jnp.arange(28, dtype=I32) // 7
    earlier = jnp.arange(28)[:, None] > jnp.arange(28)[None, :]
    nth = jnp.sum(((src[:, :, None] == src[:, None, :]) & earlier[None]).astype(I32), axis=2)
    mark = 16 + 4 * target[None, :] + leaf
    place = src * 2 + nth
    hit = place[:, :, None] == jnp.arange(32, dtype=I32)[None, None, :]
    code = jnp.sum(jnp.where(hit, mark[:, :, None], 0), axis=1).reshape(512)
    mine = lax.dynamic_slice_in_dim(src, i, 1, 0)[0]
    mine_nth = lax.dynamic_slice_in_dim(nth, i, 1, 0)[0]
    near_at = (((x - mine // 4) % 4) * 4 + (z - mine % 4) % 4) * 2 + mine_nth
    f = lax.dynamic_slice_in_dim(far, (o * 16 + i) * 4, 4, 0).reshape(32)
    fo = f // 64
    far_at = (((y - fo // 2) % 4) * 2 + (c + fo) % 2 - 1) * 4 + f % 4
    return code.astype(I32), near_at.astype(I32), far_at.astype(I32)


def shards(points, charges, interp, order, near, far, skel):
    axes = ("outer", "inner")
    code, near_at, far_at = tables(near, far)
    rank = rank_rows(order).reshape(ROWS)
    sent = pack_rows(rank, order, points, charges)
    got = lax.all_to_all(sent, axes, split_axis=0, concat_axis=0, tiled=True)
    pos = got[:, 16:32, DIM].astype(I32).reshape(ROWS)
    blk, fblk, tgt, stgt = place_rows(pos, skel, got, interp)
    pot = exchange(code, near_at, far_at, blk, fblk, tgt, stgt, interp)
    back = gather_rows(pos, pot).reshape(DEVS, 16, RHS)
    back = lax.all_to_all(back, axes, split_axis=0, concat_axis=0, tiled=True)
    return gather_rows(rank, back.reshape(ROWS, RHS))


def solution(mesh):
    rows = P(("outer", "inner"), None)
    return jax.shard_map(
        shards,
        mesh=mesh,
        in_specs=(rows, rows, rows, P(("outer", "inner")), P(), P(), rows),
        out_specs=rows,
        check_vma=False,
    )
```

time: 526 us -> 241 us (0.46); the launches traced: 516 us -> 240 us
  Pallas kernels: 0 us -> 166 us
  waiting for transfers between devices: 165 us -> 25.3 us
  local copies, waits for them, and re-layouts: 142 us -> 5.24 us
  matrix products: 115 us -> 0 us
  other arithmetic: 35.1 us -> 4.59 us
  blocking collectives: 0 us -> 27.3 us
  starting transfers between devices: 34.8 us -> 11.5 us
  between operations: 13.9 us -> 0.11 us
  loops' own time: 10.6 us -> 0 us
    pallas_call x0 -> x6, Pallas kernels: none -> 166 us  [the longest x1 126 us: exchange(): pl.pallas_call(exchange_kernel, out_shape=jax.ShapeDtypeStruct((ROWS, RHS...]
    all_gather x2 -> x0, waiting for transfers between devices: 146 us -> none  [in_one_piece(): lax.all_gather(both, axis, axis=dim, tiled=True)]
    dot_general x18 -> x0, matrix products: 115 us -> none  [the longest x8 63.5 us: apply_tile(): jnp.dot(kernel, source_chg, precision=lax.Precision.HIGHEST, preferred_el...]
    gather x15 -> x0, local copies, waits for them, and re-layouts: 102 us -> none  [the longest x2 17.3 us: shards(): skel_pts = jnp.take_along_axis(leaf_pts, skel[:, :, None], axis=1)]
    split x4 -> x0, local copies, waits for them, and re-layouts: 28 us -> none  [in_one_piece(): jnp.split(lax.all_gather(both, axis, axis=dim, tiled=True), ends, axis=al...]
    all_to_all x0 -> x1, blocking collectives: none -> 27.3 us  [shards(): back = lax.all_to_all(back, axes, split_axis=0, concat_axis=0, tiled=True)]
    all_to_all x4 -> x1, starting transfers between devices: 34.3 us -> 11.5 us  [shards(): got = lax.all_to_all(sent, axes, split_axis=0, concat_axis=0, tiled=True)]
    sort x3 -> x0, other arithmetic: 16 us -> none  [the longest x1 5.89 us: shards(): sorter = jnp.argsort(order)]
  transfers between devices with their start and end apart: 6 -> 1, of which waited for: 4 -> 1; matrix products, arithmetic and copies ran while one was open for 22% -> 2% of each run, Pallas kernels for 0% -> 0%
where the time goes in v1:
time: 241 us; the launch traced here: 240 us
  Pallas kernels  166 us (69%)
  blocking collectives  27.3 us (11%)
  waiting for transfers between devices  25.3 us (10%)
  starting transfers between devices  11.5 us (5%)
  local copies, waits for them, and re-layouts  5.24 us (2%)
  other arithmetic  4.59 us (2%)
    pallas_call x1, Pallas kernels, exchange(): pl.pallas_call(exchange_kernel, out_shape=jax.ShapeDtypeStruct((ROWS, RHS...  126 us
    all_to_all x1, blocking collectives, shards(): back = lax.all_to_all(back, axes, split_axis=0, concat_axis=0, tiled=True)  27.3 us
    all_to_all x1, waiting for transfers between devices, shards(): got = lax.all_to_all(sent, axes, split_axis=0, concat_axis=0, tiled=True)  25.3 us
    pallas_call x1, Pallas kernels, pack_rows(): pl.pallas_call(send_kernel, out_shape=jax.ShapeDtypeStruct((DEVS, 32, 128...  17.3 us
    pallas_call x1, Pallas kernels, place_rows(): pl.pallas_call(place_kernel, out_shape=[jax.ShapeDtypeStruct((2, 4, BLK,...  12.6 us
    all_to_all x1, starting transfers between devices, shards(): got = lax.all_to_all(sent, axes, split_axis=0, concat_axis=0, tiled=True)  11.5 us
    pallas_call x2, Pallas kernels, gather_rows(): pl.pallas_call(gather_kernel, out_shape=jax.ShapeDtypeStruct((ROWS, RHS),...  8.85 us
  transfers between devices with their start and end apart: 1, of which 1 were waited for; matrix products, arithmetic and copies ran while one was open for 2% of the time, Pallas kernels for 0%

profile of v1, /device:TPU:1, one launch (start us, length us, event | category | flops | bytes accessed | tf_op | source)
XLA Modules:
  0.0 240.0 jit_solution(17567972179102650814)
XLA Ops:
  0.0 0.0 copy-start
  0.0 1.8 shard_map.73
  1.8 2.4 copy.21.pts_ref
  4.2 17.3 %shard_map.74 = f32[128,32,128]{2,1,0:T(8,128)} custom-call(s32[2048]{0:T(1024)} %bitcast.6, s32[16,128]{1,0:T(8,128)} %bitcast.9, f32[2048,64]{1,0:T(8,128)} %copy.21.pts_ref, f32[2048,128]{1,0:T(8,128)} %chg_ref.1), custom_call_target="tpu_custom_call" | custom-call | tf_op jit(solution)/shard_map/pallas_call | solution.py:102
  21.4 11.5 %all-to-all-start = ((f32[128,32,128]{2,1,0:T(8,128)}), f32[128,32,128]{2,1,0:T(8,128)S(1)}, u32[]{:S(2)}, u32[]{:S(2)}) async-start(f32[128,32,128]{2,1,0:T(8,128)} %shard_map.74), calls=%async_computation | async-start | bytes 4194304 | tf_op jit(solution)/shard_map/all_to_all | solution.py:500
  33.0 0.0 copy-done
  33.0 0.1 constant_dynamic-slice_fusion.1
  33.1 0.8 constant_dynamic-slice_fusion
  33.8 0.1 copy.28
  33.9 0.1 reshape.183
  34.0 0.1 copy.22
  34.1 0.1 reshape.181
  34.2 0.1 copy.23
  34.3 0.1 add_select_fusion.1
  34.3 0.1 copy.27
  34.4 0.6 convert_reduce_fusion
  35.1 0.2 select_reduce_fusion
  35.3 0.7 reshape.182.code
  36.0 0.2 dynamic-slice_reduce_fusion
  36.1 0.6 fusion.7.far_at
  36.8 0.5 multiply_add_fusion.1.near_at
  37.3 25.3 %all-to-all-done.got_ref = f32[128,32,128]{2,1,0:T(8,128)S(1)} async-done(((f32[128,32,128]{2,1,0:T(8,128)}), f32[128,32,128]{2,1,0:T(8,128)S(1)}, u32[]{:S(2)}, u32[]{:S(2)}) %all-to-all-start) | async-done | bytes 2097184 | tf_op jit(solution)/shard_map/all_to_all | solution.py:500
  62.6 0.0 copy-start.1
  62.6 2.5 %fusion = s32[128,16]{1,0:T(8,128)S(1)} fusion(f32[128,32,128]{2,1,0:T(8,128)S(1)} %all-to-all-done.got_ref), kind=kLoop, calls=%fused_computation.1 | loop fusion | flops 2048 | bytes 16384 | tf_op jit(solution)/shard_map/convert_element_type | solution.py:501
  65.1 0.7 convert_element_type.11.pos_ref.idx_ref
  65.8 0.0 copy-done.1
  65.8 12.6 %shard_map.75 = (f32[2,4,384,128]{3,2,1,0:T(8,128)}, f32[4,384,128]{2,1,0:T(8,128)}, bf16[4,512,256]{2,1,0:T(8,128)(2,1)}, bf16[4,256,256]{2,1,0:T(8,128)(2,1)}) custom-call(s32[2048]{0:T(1024)} %convert_element_type.11.pos_ref.idx_ref, s32[4,256]{1,0:T(4,128)} %skel_ref.1, f32[128,32,128]{2,1,0:T(8,128)} %copy-done.1, f32[2048,256]{1,0:T(8,128)} %interp.1), custom_call_target="tpu_custom_call" | custom-call | tf_op jit(solution)/shard_map/pallas_call | solution.py:163
  78.3 125.6 %shard_map.76.src_ref = f32[2048,128]{1,0:T(8,128)} custom-call(s32[512]{0:T(512)} %reshape.182.code, s32[28]{0:T(128)} %multiply_add_fusion.1.near_at, s32[32]{0:T(128)} %fusion.7.far_at, f32[2,4,384,128]{3,2,1,0:T(8,128)} %get-tuple-element.9.blk, f32[4,384,128]{2,1,0:T(8,128)} %get-tuple-element.10.fblk, bf16[4,512,256]{2,1,0:T(8,128)(2,1)} %get-tuple-element.11.tgt, ...), custom_call_target="tpu_custom_call" | custom-call | tf_op jit(solution)/shard_map/pallas_call | solution.py:426
  203.9 4.4 %shard_map.77 = f32[2048,128]{1,0:T(8,128)} custom-call(s32[2048]{0:T(1024)} %convert_element_type.11.pos_ref.idx_ref, f32[2048,128]{1,0:T(8,128)} %shard_map.76.src_ref), custom_call_target="tpu_custom_call" | custom-call | tf_op jit(solution)/shard_map/pallas_call | solution.py:464
  208.3 27.3 %all_to_all.10 = f32[128,16,128]{2,1,0:T(8,128)} all-to-all(f32[128,16,128]{2,1,0:T(8,128)} %bitcast.4), channel_id=1, replica_groups=mesh['outer'=8,'inner'=16] {'outer','inner'}, dimensions={0} | all-to-all | bytes 2097152 | tf_op jit(solution)/shard_map/all_to_all | solution.py:505
  235.6 4.4 %shard_map.78 = f32[2048,128]{1,0:T(8,128)} custom-call(s32[2048]{0:T(1024)} %bitcast.7, f32[2048,128]{1,0:T(8,128)} %bitcast.5), custom_call_target="tpu_custom_call" | custom-call | tf_op jit(solution)/shard_map/pallas_call | solution.py:464
  (4 shorter events, 0.0 us)
Async XLA Ops:
  0.0 33.0 %copy-start = (s32[512,8]{0,1:T(8,128)S(1)}, s32[512,8]{0,1:T(8,128)}, u32[]{:S(2)}) copy-start(s32[512,8]{0,1:T(8,128)} %param.11) | copy-start | bytes 49156
  21.4 41.1 %all-to-all-start = ((f32[128,32,128]{2,1,0:T(8,128)}), f32[128,32,128]{2,1,0:T(8,128)S(1)}, u32[]{:S(2)}, u32[]{:S(2)}) async-start(f32[128,32,128]{2,1,0:T(8,128)} %shard_map.74), calls=%async_computation | async-start | bytes 4194304 | tf_op jit(solution)/shard_map/all_to_all | solution.py:500
  62.6 3.2 %copy-start.1 = (f32[128,32,128]{2,1,0:T(8,128)}, f32[128,32,128]{2,1,0:T(8,128)S(1)}, u32[]{:S(2)}) copy-start(f32[128,32,128]{2,1,0:T(8,128)S(1)} %all-to-all-done.got_ref) | copy-start | bytes 6291460

commit v2 on v1

--- a/solution.py
+++ b/solution.py
@@ -52,61 +52,61 @@
     return hi, mid, rest - mid
 
 
-def rank_kernel(order_ref, rank_ref):
+def rank_kernel(order_ref, rank_ref, slot_ref):
     sub = lax.broadcasted_iota(I32, (128, 128), 0)
     lane = lax.broadcasted_iota(I32, (128, 128), 1)
     before = (sub < lane).astype(F32).astype(BF16)
     ones = jnp.ones((128, 128), BF16)
     base = jnp.zeros((128, 128), F32)
     for r in range(ROWS // 128):
-        owner = order_ref[r : r + 1, :] // ROWS
+        owner = order_ref[r : r + 1, :] >> 11
         hit = (sub == owner).astype(F32)
         hit16 = hit.astype(BF16)
         seen = dot(hit16, before) + base
         base = base + dot(hit16, ones)
         count = jnp.sum(hit * seen, axis=0, keepdims=True)
-        rank_ref[r : r + 1, :] = owner * 16 + count.astype(I32)
+        nth = count.astype(I32)
+        rank_ref[r : r + 1, :] = owner * 16 + nth
+        slot_ref[r : r + 1, :] = owner * 32 + nth
 
 
 def rank_rows(order):
     return pl.pallas_call(
         rank_kernel,
-        out_shape=jax.ShapeDtypeStruct((ROWS // 128, 128), I32),
+        out_shape=[jax.ShapeDtypeStruct((ROWS // 128, 128), I32)] * 2,
         in_specs=[vspec()],
-        out_specs=vspec(),
+        out_specs=[vspec()] * 2,
     )(order.reshape(ROWS // 128, 128))
 
 
-def send_kernel(rank_ref, order_ref, pts_ref, chg_ref, sent_ref, wide):
-    lane = lax.broadcasted_iota(I32, (128, 128), 1)
+def send_kernel(slot_ref, order_ref, pts_ref, chg_ref, sent_ref, wide):
     for r in range(ROWS // 128):
-        rows = pl.ds(r * 128, 128)
-        wide[rows, 0:DIM] = pts_ref[rows, :]
-        pos = (order_ref[r : r + 1, :] % ROWS).astype(F32)
-        column = jnp.transpose(jnp.broadcast_to(pos, (128, 128)))
-        wide[rows, DIM:128] = column[:, 0:DIM]
+        pos = (order_ref[r : r + 1, :] & (ROWS - 1)).astype(F32)
+        both = jnp.concatenate([pts_ref[:, r * 128 : (r + 1) * 128], jnp.broadcast_to(pos, (DIM, 128))], axis=0)
+        wide[r * 128 : (r + 1) * 128, :] = jnp.transpose(both)
 
     def body(b, carry):
+        first = pl.multiple_of(b * 16, 16)
+        to = [slot_ref[first + u] for u in range(16)]
+        chg = [chg_ref[pl.ds(first + u, 1), :] for u in range(16)]
+        pts = [wide[pl.ds(first + u, 1), :] for u in range(16)]
         for u in range(16):
-            n = b * 16 + u
-            to = rank_ref[n]
-            dev, row = to // 16, to % 16
-            sent_ref[dev, pl.ds(row, 1), :] = chg_ref[pl.ds(n, 1), :]
-            sent_ref[dev, pl.ds(row + 16, 1), :] = wide[pl.ds(n, 1), :]
+            sent_ref[pl.ds(to[u], 1), :] = chg[u]
+            sent_ref[pl.ds(to[u] + 16, 1), :] = pts[u]
         return carry
 
     lax.fori_loop(0, ROWS // 16, body, 0)
 
 
-def pack_rows(rank, order, points, charges):
+def pack_rows(slot, order, points, charges):
     return pl.pallas_call(
         send_kernel,
-        out_shape=jax.ShapeDtypeStruct((DEVS, 32, 128), F32),
+        out_shape=jax.ShapeDtypeStruct((DEVS * 32, 128), F32),
         in_specs=[sspec(), vspec(), vspec(), vspec()],
         out_specs=vspec(),
         scratch_shapes=[pltpu.VMEM((ROWS, 128), F32)],
         compiler_params=pltpu.CompilerParams(vmem_limit_bytes=VMEM_LIMIT),
-    )(rank, order.reshape(ROWS // 128, 128), points, charges)
+    )(slot, order.reshape(ROWS // 128, 128), points.T, charges)
 
 
 def target_operand(x):
@@ -123,19 +123,21 @@
 
 def place_kernel(pos_ref, skel_ref, got_ref, interp_ref, blk_ref, fblk_ref, tgt_ref, stgt_ref, pts, chg, sk):
     def place(b, carry):
+        at = [pos_ref[b * 16 + u] for u in range(16)]
+        c = [got_ref[b, u : u + 1, :] for u in range(16)]
+        p = [got_ref[b, 16 + u : 17 + u, :] for u in range(16)]
         for u in range(16):
-            at = pos_ref[b * 16 + u]
-            chg[pl.ds(at, 1), :] = got_ref[b, u : u + 1, :]
-            pts[pl.ds(at, 1), :] = got_ref[b, 16 + u : 17 + u, :]
+            chg[pl.ds(at[u], 1), :] = c[u]
+            pts[pl.ds(at[u], 1), :] = p[u]
         return carry
 
     lax.fori_loop(0, DEVS, place, 0)
 
     def leaf(g, carry):
         def pick(b, inner):
+            rows = [pts[pl.ds(g * LEAF + skel_ref[g, b * 16 + u], 1), :] for u in range(16)]
             for u in range(16):
-                q = b * 16 + u
-                sk[pl.ds(q, 1), :] = pts[pl.ds(g * LEAF + skel_ref[g, q], 1), :]
+                sk[pl.ds(b * 16 + u, 1), :] = rows[u]
             return inner
 
         lax.fori_loop(0, 16, pick, 0)
@@ -193,24 +195,22 @@
     if scale is not None:
         chg = chg * scale
     ch, cl = hi_lo(chg)
-    return right, jnp.concatenate([ch, cl], axis=1), ch
+    return right, jnp.concatenate([ch, cl], axis=1)
 
 
 def tile(target, operand):
-    right, both, ch = operand
+    right, both = operand
+    n = target.shape[0]
     g = jnp.exp2(dot(target, right))
     gh, gl = hi_lo(g)
-    wide = dot(gh, both)
-    return wide[:, 0:128] + wide[:, 128:256] + dot(gl, ch)
-
-
-STEP = 128
+    wide = dot(jnp.concatenate([gh, gl], axis=0), both)
+    return wide[:n, 0:128] + (wide[:n, 128:256] + wide[n:, 0:128])
 
 
 def exchange_kernel(
     code, near_at, far_at, blk, fblk, tgt, stgt, interp, pot,
     p1a1, p1a2, p1a3, p1b1, p1b2, p1b3, sb, p2, p3, fb, ob,
-    s1, r1, s2, r2, s3, r3, sf, rf,
+    s1, r1, s2, r2, s3, r3, s4, r4, sf, rf,
 ):
     o, i = lax.axis_index("outer"), lax.axis_index("inner")
     y, c, x, z = o // 2, o % 2, i // 4, i % 4
@@ -253,7 +253,13 @@
         return copy(src, p1[h][2].at[part], s1.at[h, 2 + k], r1.at[h, 2 + k], first(h, 1 if k == 0 else -1))
 
     def slots(h, d, k):
-        return copy(sb.at[h, d, k], p2.at[h, d, k], s2.at[h, d, k], r2.at[h, d, k], second(h, 1 if k == 0 else -1))
+        two = pl.ds(0, 2)
+        to = second(h, 1 if k == 0 else -1)
+        return copy(sb.at[h, d, k, two], p2.at[h, d, k, two], s2.at[h, d, k], r2.at[h, d, k], to)
+
+    def ahead(h, d, k):
+        to = second(h, 1 if k == 0 else -1)
+        return copy(sb.at[h, d, k, 2], p2.at[h, d, k, 2], s4.at[h, d, k], r4.at[h, d, k], to)
 
     def relay(h, d, k):
         return copy(p2.at[h, d, k, 2], p3.at[h, d, k], s3.at[h, d, k], r3.at[h, d, k], second(h, 1 if k == 0 else -1))
@@ -278,20 +284,19 @@
     def fill(h, d):
         src = off(h, -d, 0)
         for k in range(2):
-            for slot in range(3):
+            for slot in (2, 0, 1):
                 dest = off(h, 0, (1 if k == 0 else -1) if slot < 2 else 2)
                 leaf = leaf_code(dest, src, slot if slot < 2 else k) % 4
                 if d == 0:
                     sb[h, d, k, slot] = blk[h, leaf]
                 else:
                     sb[h, d, k, slot] = p1[h][d][leaf]
+                if slot == 2:
+                    ahead(h, d, k).start()
             slots(h, d, k).start()
 
-    def add_tile(block, g, scale, at, n=LEAF):
-        operand = source_operand(block, scale)
-        for r in range(0, n, STEP):
-            rows = pl.ds(r, STEP)
-            ob[at, rows, :] += tile(tgt[g, rows, :], operand)
+    def add_tile(block, g, scale, at):
+        ob[at] += tile(tgt[g], source_operand(block, scale))
 
     def slot_tiles(h, d, e, which):
         dx, dz = (d, e) if h == 0 else (e, d)
@@ -344,44 +349,17 @@
         for h in range(2):
             slot_tiles(h, d, 0, [(j, lambda leaf, b=p1[h][d]: b[leaf]) for j in range(2)])
 
-    first_tiles(1)
-    far_copies["up2"].wait_recv()
-    far_copies["down2"].wait_recv()
-    far_copies["side2"].start()
-    for h in range(2):
-        onward(h, 0).wait_recv()
-        onward(h, 1).wait_recv()
-        fill(h, 2)
-    first_tiles(3)
-
-    def arrive(d):
+    def pass_on(d):
+        for h in range(2):
+            for k in range(2):
+                ahead(h, d, k).wait_recv()
+                relay(h, d, k).start()
+
+    def second_tiles(d):
         for h in range(2):
             for k in range(2):
                 slots(h, d, k).wait_recv()
-                relay(h, d, k).start()
-
-    def second_tiles(d):
-        for h in range(2):
-            for k in range(2):
                 slot_tiles(h, d, 1 if k == 0 else 3, [(j, lambda leaf, k=k, j=j: p2[h, d, k, j]) for j in range(2)])
-
-    arrive(0)
-    first_tiles(2)
-    second_tiles(0)
-    for name in ("side1", "side3", "side2"):
-        far_copies[name].wait_recv()
-
-    def far_leaf(g, carry):
-        def one(k, q):
-            operand = source_operand(fb[far_at[g * 8 + k]], None)
-            return q + tile(stgt[g], operand)
-
-        q = lax.fori_loop(0, 8, one, jnp.zeros((HALF, 128), F32))
-        rows = pl.ds(pl.multiple_of(g * LEAF, LEAF), LEAF)
-        pot[rows, :] += dot3(interp[rows, :], q)
-        return carry
-
-    lax.fori_loop(0, 4, far_leaf, 0)
 
     def relay_tiles(d):
         for h in range(2):
@@ -389,12 +367,39 @@
                 relay(h, d, k).wait_recv()
             slot_tiles(h, d, 2, [(j, lambda leaf, j=j: p3[h, d, j]) for j in range(2)])
 
-    arrive(1)
+    def far_leaf(g):
+        def one(k, q):
+            operand = source_operand(fb[far_at[g * 8 + k]], None)
+            return q + tile(stgt[g], operand)
+
+        q = lax.fori_loop(0, 8, one, jnp.zeros((HALF, 128), F32))
+        rows = pl.ds(g * LEAF, LEAF)
+        pot[rows, :] += dot3(interp[rows, :], q)
+
+    pass_on(0)
+    for h in range(2):
+        onward(h, 0).wait_recv()
+        onward(h, 1).wait_recv()
+        fill(h, 2)
+    far_copies["up2"].wait_recv()
+    far_copies["down2"].wait_recv()
+    far_copies["side2"].start()
+    first_tiles(1)
+    first_tiles(3)
+    for name in ("side1", "side3", "side2"):
+        far_copies[name].wait_recv()
+    second_tiles(0)
+    pass_on(1)
+    far_leaf(0)
+    pass_on(3)
+    far_leaf(1)
+    pass_on(2)
+    first_tiles(2)
+    far_leaf(2)
+    far_leaf(3)
     second_tiles(1)
-    arrive(3)
     second_tiles(3)
     relay_tiles(0)
-    arrive(2)
     second_tiles(2)
     relay_tiles(1)
     relay_tiles(3)
@@ -416,6 +421,7 @@
             onward(h, k).wait_send()
             for d in range(4):
                 slots(h, d, k).wait_send()
+                ahead(h, d, k).wait_send()
                 relay(h, d, k).wait_send()
     for one in far_copies.values():
         one.wait_send()
@@ -437,10 +443,9 @@
             pltpu.VMEM((32, LEAF, 128), F32),
             dma((2, 4)),
             dma((2, 4)),
-            dma((2, 4, 2)),
-            dma((2, 4, 2)),
-            dma((2, 4, 2)),
-            dma((2, 4, 2)),
+        ]
+        + [dma((2, 4, 2))] * 6
+        + [
             dma((8,)),
             dma((8,)),
         ],
@@ -452,9 +457,10 @@
 
 def gather_kernel(idx_ref, src_ref, dst_ref):
     def body(b, carry):
+        first = pl.multiple_of(b * 16, 16)
+        rows = [src_ref[pl.ds(idx_ref[first + u], 1), :] for u in range(16)]
         for u in range(16):
-            n = b * 16 + u
-            dst_ref[pl.ds(n, 1), :] = src_ref[pl.ds(idx_ref[n], 1), :]
+            dst_ref[pl.ds(first + u, 1), :] = rows[u]
         return carry
 
     lax.fori_loop(0, ROWS // 16, body, 0)
@@ -495,8 +501,8 @@
 def shards(points, charges, interp, order, near, far, skel):
     axes = ("outer", "inner")
     code, near_at, far_at = tables(near, far)
-    rank = rank_rows(order).reshape(ROWS)
-    sent = pack_rows(rank, order, points, charges)
+    rank, slot = (v.reshape(ROWS) for v in rank_rows(order))
+    sent = pack_rows(slot, order, points, charges).reshape(DEVS, 32, 128)
     got = lax.all_to_all(sent, axes, split_axis=0, concat_axis=0, tiled=True)
     pos = got[:, 16:32, DIM].astype(I32).reshape(ROWS)
     blk, fblk, tgt, stgt = place_rows(pos, skel, got, interp)

time: 241 us -> 204 us (0.85)
  Pallas kernels: 166 us -> 135 us
  blocking collectives: 27.3 us -> 24.4 us
    pallas_call x1, Pallas kernels: 126 us -> 106 us  [exchange(): pl.pallas_call(exchange_kernel, out_shape=jax.ShapeDtypeStruct((ROWS, RHS...]
    pallas_call x2, Pallas kernels: 19.1 us -> 7.32 us  [the longest x1 5.52 us: pack_rows(): pl.pallas_call(send_kernel, out_shape=jax.ShapeDtypeStruct((DEVS * 32, 12...]
    all_to_all x1, blocking collectives: 27.3 us -> 24.4 us  [shards(): back = lax.all_to_all(back, axes, split_axis=0, concat_axis=0, tiled=True)]
where the time goes in v2:
time: 204 us
  Pallas kernels  135 us (66%)
  waiting for transfers between devices  25.3 us (12%)
  blocking collectives  24.4 us (12%)
  starting transfers between devices  11.5 us (6%)
  other arithmetic  4.59 us (2%)
  local copies, waits for them, and re-layouts  2.89 us (1%)
    pallas_call x1, Pallas kernels, exchange(): pl.pallas_call(exchange_kernel, out_shape=jax.ShapeDtypeStruct((ROWS, RHS...  106 us
    all_to_all x1, waiting for transfers between devices, shards(): got = lax.all_to_all(sent, axes, split_axis=0, concat_axis=0, tiled=True)  25.3 us
    all_to_all x1, blocking collectives, shards(): back = lax.all_to_all(back, axes, split_axis=0, concat_axis=0, tiled=True)  24.4 us
    pallas_call x1, Pallas kernels, place_rows(): pl.pallas_call(place_kernel, out_shape=[jax.ShapeDtypeStruct((2, 4, BLK,...  12.6 us
    all_to_all x1, starting transfers between devices, shards(): got = lax.all_to_all(sent, axes, split_axis=0, concat_axis=0, tiled=True)  11.5 us
    pallas_call x2, Pallas kernels, gather_rows(): pl.pallas_call(gather_kernel, out_shape=jax.ShapeDtypeStruct((ROWS, RHS),...  8.85 us
    pallas_call x1, Pallas kernels, pack_rows(): pl.pallas_call(send_kernel, out_shape=jax.ShapeDtypeStruct((DEVS * 32, 12...  5.52 us
  transfers between devices with their start and end apart: 1, of which 1 were waited for; matrix products, arithmetic and copies ran while one was open for 2% of the time, Pallas kernels for 0%

profile of v2, /device:TPU:1, one launch (start us, length us, event | category | flops | bytes accessed | tf_op | source)
XLA Modules:
  0.0 203.5 jit_solution(3774864843362801813)
XLA Ops:
  0.0 0.0 copy-start
  0.0 1.8 shard_map.73
  1.8 5.5 %shard_map.74 = f32[4096,128]{1,0:T(8,128)} custom-call(s32[2048]{0:T(1024)} %bitcast.14, s32[16,128]{1,0:T(8,128)} %bitcast.12, f32[64,2048]{1,0:T(8,128)} %bitcast.10, f32[2048,128]{1,0:T(8,128)} %chg_ref.1), custom_call_target="tpu_custom_call" | custom-call | tf_op jit(solution)/shard_map/pallas_call | solution.py:102
  7.3 11.5 %all-to-all-start = ((f32[128,32,128]{2,1,0:T(8,128)}), f32[128,32,128]{2,1,0:T(8,128)S(1)}, u32[]{:S(2)}, u32[]{:S(2)}) async-start(f32[128,32,128]{2,1,0:T(8,128)} %bitcast.7), calls=%async_computation | async-start | bytes 4194304 | tf_op jit(solution)/shard_map/all_to_all | solution.py:506
  18.9 0.0 copy-done
  18.9 0.1 constant_dynamic-slice_fusion.1
  19.0 0.8 constant_dynamic-slice_fusion
  19.7 0.1 copy.24
  19.8 0.1 reshape.191
  19.9 0.1 copy.18
  20.0 0.1 reshape.189
  20.1 0.1 copy.19
  20.2 0.1 add_select_fusion.1
  20.3 0.1 copy.23
  20.3 0.6 convert_reduce_fusion
  21.0 0.2 select_reduce_fusion
  21.2 0.7 reshape.190.code
  21.9 0.2 dynamic-slice_reduce_fusion
  22.0 0.6 fusion.7.far_at
  22.7 0.5 multiply_add_fusion.1.near_at
  23.2 25.3 %all-to-all-done.got_ref = f32[128,32,128]{2,1,0:T(8,128)S(1)} async-done(((f32[128,32,128]{2,1,0:T(8,128)}), f32[128,32,128]{2,1,0:T(8,128)S(1)}, u32[]{:S(2)}, u32[]{:S(2)}) %all-to-all-start) | async-done | bytes 2097184 | tf_op jit(solution)/shard_map/all_to_all | solution.py:506
  48.5 0.0 copy-start.1
  48.5 2.5 %fusion = s32[128,16]{1,0:T(8,128)S(1)} fusion(f32[128,32,128]{2,1,0:T(8,128)S(1)} %all-to-all-done.got_ref), kind=kLoop, calls=%fused_computation.1 | loop fusion | flops 2048 | bytes 16384 | tf_op jit(solution)/shard_map/convert_element_type | solution.py:507
  51.0 0.7 convert_element_type.11.pos_ref.idx_ref
  51.7 0.0 copy-done.1
  51.7 12.6 %shard_map.75 = (f32[2,4,384,128]{3,2,1,0:T(8,128)}, f32[4,384,128]{2,1,0:T(8,128)}, bf16[4,512,256]{2,1,0:T(8,128)(2,1)}, bf16[4,256,256]{2,1,0:T(8,128)(2,1)}) custom-call(s32[2048]{0:T(1024)} %convert_element_type.11.pos_ref.idx_ref, s32[4,256]{1,0:T(4,128)} %skel_ref.1, f32[128,32,128]{2,1,0:T(8,128)} %copy-done.1, f32[2048,256]{1,0:T(8,128)} %interp.1), custom_call_target="tpu_custom_call" | custom-call | tf_op jit(solution)/shard_map/pallas_call | solution.py:165
  64.2 106.1 %shard_map.76.src_ref = f32[2048,128]{1,0:T(8,128)} custom-call(s32[512]{0:T(512)} %reshape.190.code, s32[28]{0:T(128)} %multiply_add_fusion.1.near_at, s32[32]{0:T(128)} %fusion.7.far_at, f32[2,4,384,128]{3,2,1,0:T(8,128)} %get-tuple-element.13.blk, f32[4,384,128]{2,1,0:T(8,128)} %get-tuple-element.14.fblk, bf16[4,512,256]{2,1,0:T(8,128)(2,1)} %get-tuple-element.15.tgt, ...), custom_call_target="tpu_custom_call" | custom-call | tf_op jit(solution)/shard_map/pallas_call | solution.py:432
  170.3 4.4 %shard_map.77 = f32[2048,128]{1,0:T(8,128)} custom-call(s32[2048]{0:T(1024)} %convert_element_type.11.pos_ref.idx_ref, f32[2048,128]{1,0:T(8,128)} %shard_map.76.src_ref), custom_call_target="tpu_custom_call" | custom-call | tf_op jit(solution)/shard_map/pallas_call | solution.py:470
  174.7 24.4 %all_to_all.10 = f32[128,16,128]{2,1,0:T(8,128)} all-to-all(f32[128,16,128]{2,1,0:T(8,128)} %bitcast.9), channel_id=1, replica_groups=mesh['outer'=8,'inner'=16] {'outer','inner'}, dimensions={0} | all-to-all | bytes 2097152 | tf_op jit(solution)/shard_map/all_to_all | solution.py:511
  199.1 4.4 %shard_map.78 = f32[2048,128]{1,0:T(8,128)} custom-call(s32[2048]{0:T(1024)} %bitcast.13, f32[2048,128]{1,0:T(8,128)} %bitcast.8), custom_call_target="tpu_custom_call" | custom-call | tf_op jit(solution)/shard_map/pallas_call | solution.py:470
  (4 shorter events, 0.0 us)
Async XLA Ops:
  0.0 18.9 %copy-start = (s32[512,8]{0,1:T(8,128)S(1)}, s32[512,8]{0,1:T(8,128)}, u32[]{:S(2)}) copy-start(s32[512,8]{0,1:T(8,128)} %param.11) | copy-start | bytes 49156
  7.3 41.2 %all-to-all-start = ((f32[128,32,128]{2,1,0:T(8,128)}), f32[128,32,128]{2,1,0:T(8,128)S(1)}, u32[]{:S(2)}, u32[]{:S(2)}) async-start(f32[128,32,128]{2,1,0:T(8,128)} %bitcast.7), calls=%async_computation | async-start | bytes 4194304 | tf_op jit(solution)/shard_map/all_to_all | solution.py:506
  48.5 3.2 %copy-start.1 = (f32[128,32,128]{2,1,0:T(8,128)}, f32[128,32,128]{2,1,0:T(8,128)S(1)}, u32[]{:S(2)}) copy-start(f32[128,32,128]{2,1,0:T(8,128)S(1)} %all-to-all-done.got_ref) | copy-start | bytes 6291460

commit v3 on v2

--- a/solution.py
+++ b/solution.py
@@ -52,61 +52,211 @@
     return hi, mid, rest - mid
 
 
-def rank_kernel(order_ref, rank_ref, slot_ref):
+def plan_kernel(order_ref, near_ref, far_ref, rank_ref, slot_ref, posmat_ref, code_ref, near_at_ref, far_at_ref):
     sub = lax.broadcasted_iota(I32, (128, 128), 0)
     lane = lax.broadcasted_iota(I32, (128, 128), 1)
     before = (sub < lane).astype(F32).astype(BF16)
     ones = jnp.ones((128, 128), BF16)
     base = jnp.zeros((128, 128), F32)
+    posmat = jnp.zeros((256, 16), F32)
     for r in range(ROWS // 128):
-        owner = order_ref[r : r + 1, :] >> 11
+        order = order_ref[r : r + 1, :]
+        owner = order >> 11
         hit = (sub == owner).astype(F32)
         hit16 = hit.astype(BF16)
         seen = dot(hit16, before) + base
         base = base + dot(hit16, ones)
-        count = jnp.sum(hit * seen, axis=0, keepdims=True)
-        nth = count.astype(I32)
+        nth = jnp.sum(hit * seen, axis=0, keepdims=True).astype(I32)
         rank_ref[r : r + 1, :] = owner * 16 + nth
         slot_ref[r : r + 1, :] = owner * 32 + nth
-
-
-def rank_rows(order):
+        pos = ((order >> 8) & 1) * 1024 + ((order >> 9) & 3) * HALF + (order & 255)
+        slot = (sub[0:16] == nth).astype(F32).astype(BF16)
+        high = (hit * (pos >> 4).astype(F32)).astype(BF16)
+        low = (hit * (pos & 15).astype(F32)).astype(BF16)
+        posmat = posmat + dot(jnp.concatenate([high, low], axis=0), slot, ((1,), (1,)))
+    posmat = 16.0 * posmat[0:128] + posmat[128:256]
+    posmat_ref[...] = jnp.concatenate([posmat, jnp.zeros((128, 112), F32)], axis=1)
+
+    o, i = lax.axis_index("outer"), lax.axis_index("inner")
+    y, c, x, z = o >> 1, o & 1, i >> 2, i & 3
+    entry = near_ref[...]
+    row = lax.broadcasted_iota(I32, entry.shape, 0)
+    g = lax.broadcasted_iota(I32, entry.shape, 1) & 3
+    src = jnp.where(row == 0, -1, (entry >> 2) & 15)
+    nth = jnp.zeros(entry.shape, I32)
+    for back in range(4):
+        other = src if back == 0 else pltpu.roll(src, back, axis=1)
+        for k in range(1, 8):
+            earlier = (row > k) if back == 0 else (g >= back)
+            nth = nth + jnp.where((other[k : k + 1, :] == src) & earlier, 1, 0)
+    place = src * 2 + nth
+    mark = 16 + 4 * g + (entry & 3)
+    want = lax.broadcasted_iota(I32, (32, entry.shape[1]), 0)
+    code = jnp.zeros(want.shape, I32)
+    for k in range(1, 8):
+        code = code + jnp.where(want == place[k : k + 1, :], mark[k : k + 1, :], 0)
+    n = code.shape[1]
+    code = code + pltpu.roll(code, n - 1, axis=1)
+    code_ref[...] = code + pltpu.roll(code, n - 2, axis=1)
+    near_at_ref[...] = ((((x - (src >> 2)) & 3) * 4 + ((z - src) & 3)) * 2 + nth) & 31
+    f = far_ref[...]
+    fo = f >> 6
+    far_at_ref[...] = ((((y - (fo >> 1)) & 3) * 2 + ((c + fo) & 1)) - 1) * 4 + (f & 3)
+
+
+def make_plan(order, near, far):
+    leaves = near.shape[0]
+    sd = jax.ShapeDtypeStruct
     return pl.pallas_call(
-        rank_kernel,
-        out_shape=[jax.ShapeDtypeStruct((ROWS // 128, 128), I32)] * 2,
-        in_specs=[vspec()],
-        out_specs=[vspec()] * 2,
-    )(order.reshape(ROWS // 128, 128))
-
-
-def send_kernel(slot_ref, order_ref, pts_ref, chg_ref, sent_ref, wide):
+        plan_kernel,
+        out_shape=[sd((ROWS // 128, 128), I32)] * 2
+        + [sd((DEVS, 128), F32), sd((32, leaves), I32), sd((8, leaves), I32), sd((8, leaves), I32)],
+        in_specs=[vspec()] * 3,
+        out_specs=[vspec()] * 6,
+    )(order.reshape(ROWS // 128, 128), near.T, far.T)
+
+
+SENT = 25
+
+
+def send_kernel(rank_ref, slot_ref, pts_ref, chg_ref, posmat_ref, sent_ref, wide, ranked):
     for r in range(ROWS // 128):
-        pos = (order_ref[r : r + 1, :] & (ROWS - 1)).astype(F32)
-        both = jnp.concatenate([pts_ref[:, r * 128 : (r + 1) * 128], jnp.broadcast_to(pos, (DIM, 128))], axis=0)
-        wide[r * 128 : (r + 1) * 128, :] = jnp.transpose(both)
+        x = pts_ref[:, r * 128 : (r + 1) * 128]
+        wide[r * 128 : (r + 1) * 128, :] = jnp.transpose(jnp.concatenate([x, x], axis=0))
 
     def body(b, carry):
         first = pl.multiple_of(b * 16, 16)
         to = [slot_ref[first + u] for u in range(16)]
+        at = [rank_ref[first + u] for u in range(16)]
         chg = [chg_ref[pl.ds(first + u, 1), :] for u in range(16)]
         pts = [wide[pl.ds(first + u, 1), :] for u in range(16)]
         for u in range(16):
             sent_ref[pl.ds(to[u], 1), :] = chg[u]
-            sent_ref[pl.ds(to[u] + 16, 1), :] = pts[u]
+            ranked[pl.ds(at[u], 1), :] = pts[u]
         return carry
 
     lax.fori_loop(0, ROWS // 16, body, 0)
-
-
-def pack_rows(slot, order, points, charges):
+    left = lax.broadcasted_iota(I32, (8, 128), 1) < DIM
+
+    def pack(b, carry):
+        for u in range(8):
+            d = b * 8 + u
+            low = ranked[pl.ds(pl.multiple_of(d * 16, 8), 8), :]
+            high = ranked[pl.ds(pl.multiple_of(d * 16 + 8, 8), 8), :]
+            sent_ref[pl.ds(pl.multiple_of(d * 32 + 16, 8), 8), :] = jnp.where(left, low, high)
+            sent_ref[pl.ds(d * 32 + 24, 1), :] = posmat_ref[pl.ds(d, 1), :]
+        return carry
+
+    lax.fori_loop(0, DEVS // 8, pack, 0)
+
+
+def pack_rows(rank, slot, points, charges, posmat):
     return pl.pallas_call(
         send_kernel,
         out_shape=jax.ShapeDtypeStruct((DEVS * 32, 128), F32),
-        in_specs=[sspec(), vspec(), vspec(), vspec()],
+        in_specs=[sspec(), sspec(), vspec(), vspec(), vspec()],
         out_specs=vspec(),
-        scratch_shapes=[pltpu.VMEM((ROWS, 128), F32)],
+        scratch_shapes=[pltpu.VMEM((ROWS, 128), F32)] * 2,
         compiler_params=pltpu.CompilerParams(vmem_limit_bytes=VMEM_LIMIT),
-    )(slot, order.reshape(ROWS // 128, 128), points.T, charges)
+    )(rank, slot, points.T, charges, posmat)
+
+
+def peer(t):
+    o, i = lax.axis_index("outer"), lax.axis_index("inner")
+    y, c, x, z = o >> 1, o & 1, i >> 2, i & 3
+    a, b, e, other = t & 3, (t >> 2) & 3, (t >> 4) & 3, t >> 6
+    return ((((y + a) & 3) << 1) | (c ^ other), (((x + a + b) & 3) << 2) | ((z + e + 3 * a) & 3))
+
+
+def greet_all():
+    barrier = pltpu.get_barrier_semaphore()
+
+    def greet(t, carry):
+        pl.semaphore_signal(barrier, inc=1, device_id=peer(t), device_id_type=MESH)
+        return carry
+
+    lax.fori_loop(1, DEVS, greet, 0)
+    pl.semaphore_wait(barrier, DEVS - 1)
+
+
+def out_kernel(src, dst, pos, send, recv, own):
+    me = lax.axis_index("outer") * 16 + lax.axis_index("inner")
+    rows = pl.ds(0, SENT)
+    keep = pltpu.make_async_copy(src.at[me, rows], dst.at[me, rows], own)
+    keep.start()
+    greet_all()
+
+    def go(t, carry):
+        to = peer(t)
+        pltpu.make_async_remote_copy(
+            src_ref=src.at[to[0] * 16 + to[1], rows], dst_ref=dst.at[me, rows], send_sem=send, recv_sem=recv,
+            device_id=to, device_id_type=MESH,
+        ).start()
+        return carry
+
+    lax.fori_loop(1, DEVS, go, 0)
+    most = pl.ds(0, DEVS - 1)
+    whole = pltpu.make_async_remote_copy(
+        src_ref=src.at[most, rows], dst_ref=dst.at[most, rows], send_sem=send, recv_sem=recv,
+        device_id=peer(1), device_id_type=MESH,
+    )
+    keep.wait()
+    whole.wait_recv()
+    pos[...] = dst[:, 24, :].astype(I32)
+    whole.wait_send()
+
+
+def rows_out(sent):
+    dma = pltpu.SemaphoreType.DMA
+    return pl.pallas_call(
+        out_kernel,
+        out_shape=[jax.ShapeDtypeStruct((DEVS, 32, 128), F32), jax.ShapeDtypeStruct((DEVS, 128), I32)],
+        in_specs=[vspec()],
+        out_specs=[vspec()] * 2,
+        scratch_shapes=[dma, dma, dma],
+        compiler_params=pltpu.CompilerParams(vmem_limit_bytes=VMEM_LIMIT, collective_id=1, has_side_effects=True),
+    )(sent.reshape(DEVS, 32, 128))
+
+
+def place_kernel(pos_ref, got_ref, blk_ref, pts_ref, turned):
+    def turn(b, carry):
+        for u in range(8):
+            d = b * 8 + u
+            rows = got_ref[pl.ds(pl.multiple_of(d * 32 + 16, 8), 8), :]
+            turned[pl.ds(pl.multiple_of(d * 8, 8), 8), :] = pltpu.roll(rows, DIM, axis=1)
+        return carry
+
+    lax.fori_loop(0, DEVS // 8, turn, 0)
+
+    def place(b, carry):
+        at = [pos_ref[b, u] for u in range(16)]
+        row = [a + ((a >> 8) << 7) for a in at]
+        base = pl.multiple_of(b * 32, 32)
+        half = pl.multiple_of(b * 8, 8)
+        c = [got_ref[pl.ds(base + u, 1), :] for u in range(16)]
+        p = [got_ref[pl.ds(base + 16 + u, 1), :] for u in range(8)] + [turned[pl.ds(half + u, 1), :] for u in range(8)]
+        for u in range(16):
+            blk_ref[pl.ds(row[u], 1), :] = c[u]
+            pts_ref[pl.ds(at[u], 1), :] = p[u]
+        return carry
+
+    lax.fori_loop(0, DEVS, place, 0)
+    for k in range(8):
+        xt = jnp.transpose(pts_ref[k * HALF : (k + 1) * HALF, :])
+        blk_ref[k * BLK + HALF : k * BLK + HALF + 64, :] = xt[0:64, 0:128]
+        blk_ref[k * BLK + HALF + 64 : (k + 1) * BLK, :] = xt[0:64, 128:256]
+
+
+def place_rows(pos, got):
+    blk, pts = pl.pallas_call(
+        place_kernel,
+        out_shape=[jax.ShapeDtypeStruct((8 * BLK, 128), F32), jax.ShapeDtypeStruct((ROWS, 128), F32)],
+        in_specs=[sspec(), vspec()],
+        out_specs=[vspec()] * 2,
+        scratch_shapes=[pltpu.VMEM((DEVS * 8, 128), F32)],
+        compiler_params=pltpu.CompilerParams(vmem_limit_bytes=VMEM_LIMIT),
+    )(pos, got.reshape(DEVS * 32, 128))
+    return blk.reshape(2, 4, BLK, 128), pts
 
 
 def target_operand(x):
@@ -119,66 +269,6 @@
         lane == 0, n0, jnp.where(lane == 1, n1, jnp.where(lane == 2, n2, jnp.where(lane < 6, 1.0, 0.0)))
     )
     return jnp.concatenate([hi, hi, lo, tail.astype(BF16)], axis=1)
-
-
-def place_kernel(pos_ref, skel_ref, got_ref, interp_ref, blk_ref, fblk_ref, tgt_ref, stgt_ref, pts, chg, sk):
-    def place(b, carry):
-        at = [pos_ref[b * 16 + u] for u in range(16)]
-        c = [got_ref[b, u : u + 1, :] for u in range(16)]
-        p = [got_ref[b, 16 + u : 17 + u, :] for u in range(16)]
-        for u in range(16):
-            chg[pl.ds(at[u], 1), :] = c[u]
-            pts[pl.ds(at[u], 1), :] = p[u]
-        return carry
-
-    lax.fori_loop(0, DEVS, place, 0)
-
-    def leaf(g, carry):
-        def pick(b, inner):
-            rows = [pts[pl.ds(g * LEAF + skel_ref[g, b * 16 + u], 1), :] for u in range(16)]
-            for u in range(16):
-                sk[pl.ds(b * 16 + u, 1), :] = rows[u]
-            return inner
-
-        lax.fori_loop(0, 16, pick, 0)
-        for h in range(2):
-            rows = pl.ds(pl.multiple_of(g * LEAF + h * HALF, HALF), HALF)
-            blk_ref[h, g, 0:HALF, :] = chg[rows, :]
-            x = pts[rows, :]
-            xt = jnp.transpose(x)
-            blk_ref[h, g, HALF : HALF + 64, :] = xt[0:64, 0:128]
-            blk_ref[h, g, HALF + 64 : BLK, :] = xt[0:64, 128:256]
-            tgt_ref[g, h * HALF : (h + 1) * HALF, :] = target_operand(x[:, 0:DIM])
-        s = sk[...]
-        st = jnp.transpose(s)
-        fblk_ref[g, HALF : HALF + 64, :] = st[0:64, 0:128]
-        fblk_ref[g, HALF + 64 : BLK, :] = st[0:64, 128:256]
-        stgt_ref[g] = target_operand(s[:, 0:DIM])
-        rows = pl.ds(pl.multiple_of(g * LEAF, LEAF), LEAF)
-        fblk_ref[g, 0:HALF, :] = dot3(interp_ref[rows, :], chg[rows, :], ((0,), (0,)))
-        return carry
-
-    lax.fori_loop(0, 4, leaf, 0)
-
-
-def place_rows(pos, skel, got, interp):
-    return pl.pallas_call(
-        place_kernel,
-        out_shape=[
-            jax.ShapeDtypeStruct((2, 4, BLK, 128), F32),
-            jax.ShapeDtypeStruct((4, BLK, 128), F32),
-            jax.ShapeDtypeStruct((4, LEAF, 256), BF16),
-            jax.ShapeDtypeStruct((4, HALF, 256), BF16),
-        ],
-        in_specs=[sspec(), sspec(), vspec(), vspec()],
-        out_specs=[vspec()] * 4,
-        scratch_shapes=[
-            pltpu.VMEM((ROWS, 128), F32),
-            pltpu.VMEM((ROWS, 128), F32),
-            pltpu.VMEM((HALF, 128), F32),
-        ],
-        compiler_params=pltpu.CompilerParams(vmem_limit_bytes=VMEM_LIMIT),
-    )(pos, skel, got, interp)
 
 
 def source_operand(block, scale):
@@ -208,8 +298,8 @@
 
 
 def exchange_kernel(
-    code, near_at, far_at, blk, fblk, tgt, stgt, interp, pot,
-    p1a1, p1a2, p1a3, p1b1, p1b2, p1b3, sb, p2, p3, fb, ob,
+    code, near_at, far_at, skel, blk, pts, interp, pot,
+    fblk, tgt, stgt, sk, p1a1, p1a2, p1a3, p1b1, p1b2, p1b3, sb, p2, p3, fb, ob,
     s1, r1, s2, r2, s3, r3, s4, r4, sf, rf,
 ):
     o, i = lax.axis_index("outer"), lax.axis_index("inner")
@@ -232,6 +322,7 @@
         return (((y + d + 4) % 4) * 2 + c, i)
 
     sibling = (y * 2 + 1 - c, i)
+    mine = (o * 16 + i) * 4
 
     barrier = pltpu.get_barrier_semaphore()
     peers = [first(0, 1), first(0, -1), second(0, 1), second(0, -1), along_y(1), along_y(-1), sibling]
@@ -279,7 +370,7 @@
     }
 
     def leaf_code(dest, src, j):
-        return code[(dest * 16 + src) * 2 + j]
+        return code[src * 2 + j, (o * 16 + dest) * 4]
 
     def fill(h, d):
         src = off(h, -d, 0)
@@ -309,11 +400,40 @@
     own_first(0, 1).start()
     own_first(1, 0).start()
     own_first(1, 1).start()
+    fill(0, 0)
+    fill(1, 0)
+
+    for g in range(4):
+        def pick(b, carry, g=g):
+            rows = []
+            for u in range(16):
+                q = skel[g, b * 16 + u]
+                rows.append(pts[pl.ds((q >> 8) * 1024 + g * HALF + (q & 255), 1), :])
+            for u in range(16):
+                sk[pl.ds(b * 16 + u, 1), :] = rows[u]
+            return carry
+
+        lax.fori_loop(0, 16, pick, 0)
+        skt = jnp.transpose(sk[...])
+        fblk[g, HALF : HALF + 64, :] = skt[0:64, 0:128]
+        fblk[g, HALF + 64 : BLK, :] = skt[0:64, 128:256]
+        stgt[g] = target_operand(sk[:, 0:DIM])
+        charges = jnp.zeros((HALF, RHS), F32)
+        for h in range(2):
+            tgt[g, h * HALF : (h + 1) * HALF, :] = target_operand(pts[h * 1024 + g * HALF : h * 1024 + (g + 1) * HALF, 0:DIM])
+            weights = interp[g * LEAF + h * HALF : g * LEAF + (h + 1) * HALF, :]
+            charges = charges + dot3(weights, blk[h, g, 0:HALF, :], ((0,), (0,)))
+        fblk[g, 0:HALF, :] = charges
     far_copies["up"].start()
     far_copies["down"].start()
     far_copies["own"].start()
-    fill(0, 0)
-    fill(1, 0)
+
+    def halves(g):
+        return [pl.ds(pl.multiple_of(h * 1024 + g * HALF, HALF), HALF) for h in range(2)]
+
+    def put(g, values):
+        for h, rows in enumerate(halves(g)):
+            pot[rows, :] = values[h * HALF : (h + 1) * HALF, :]
 
     def zero(t, carry):
         ob[t] = jnp.zeros((LEAF, 128), F32)
@@ -324,11 +444,10 @@
     def own(t, carry):
         g, h = t // 2, t % 2
         add_tile(blk[h, g], g, None, 0)
-        rows = pl.ds(pl.multiple_of(g * LEAF, LEAF), LEAF)
 
         @pl.when(h == 1)
         def _():
-            pot[rows, :] = ob[0]
+            put(g, ob[0])
             ob[0] = jnp.zeros((LEAF, 128), F32)
 
         return carry
@@ -369,12 +488,13 @@
 
     def far_leaf(g):
         def one(k, q):
-            operand = source_operand(fb[far_at[g * 8 + k]], None)
+            operand = source_operand(fb[far_at[k, mine + g]], None)
             return q + tile(stgt[g], operand)
 
         q = lax.fori_loop(0, 8, one, jnp.zeros((HALF, 128), F32))
-        rows = pl.ds(g * LEAF, LEAF)
-        pot[rows, :] += dot3(interp[rows, :], q)
+        more = dot3(interp[g * LEAF : (g + 1) * LEAF, :], q)
+        for h, rows in enumerate(halves(g)):
+            pot[rows, :] += more[h * HALF : (h + 1) * HALF, :]
 
     pass_on(0)
     for h in range(2):
@@ -406,11 +526,12 @@
     relay_tiles(2)
 
     def finish(g, carry):
-        rows = pl.ds(pl.multiple_of(g * LEAF, LEAF), LEAF)
-        total = pot[rows, :]
-        for k in range(7):
-            total = total + ob[near_at[g * 7 + k]]
-        pot[rows, :] = total
+        at = [near_at[k + 1, mine + g] for k in range(7)]
+        for h, rows in enumerate(halves(g)):
+            total = pot[rows, :]
+            for k in range(7):
+                total = total + ob[at[k], h * HALF : (h + 1) * HALF, :]
+            pot[rows, :] = total
         return carry
 
     lax.fori_loop(0, 4, finish, 0)
@@ -427,14 +548,20 @@
         one.wait_send()
 
 
-def exchange(code, near_at, far_at, blk, fblk, tgt, stgt, interp):
+def exchange(code, near_at, far_at, skel, blk, pts, interp):
     dma = pltpu.SemaphoreType.DMA
     return pl.pallas_call(
         exchange_kernel,
         out_shape=jax.ShapeDtypeStruct((ROWS, RHS), F32),
-        in_specs=[sspec()] * 3 + [vspec()] * 5,
+        in_specs=[sspec()] * 4 + [vspec()] * 3,
         out_specs=vspec(),
-        scratch_shapes=[pltpu.VMEM((4, BLK, 128), F32)] * 6
+        scratch_shapes=[
+            pltpu.VMEM((4, BLK, 128), F32),
+            pltpu.VMEM((4, LEAF, 256), BF16),
+            pltpu.VMEM((4, HALF, 256), BF16),
+            pltpu.VMEM((HALF, 128), F32),
+        ]
+        + [pltpu.VMEM((4, BLK, 128), F32)] * 6
         + [
             pltpu.VMEM((2, 4, 2, 3, BLK, 128), F32),
             pltpu.VMEM((2, 4, 2, 3, BLK, 128), F32),
@@ -452,7 +579,49 @@
         compiler_params=pltpu.CompilerParams(
             vmem_limit_bytes=VMEM_LIMIT, collective_id=0, has_side_effects=True
         ),
-    )(code, near_at, far_at, blk, fblk, tgt, stgt, interp)
+    )(code, near_at, far_at, skel, blk, pts, interp)
+
+
+def back_kernel(pos, pot, dst, buf, send, recv):
+    me = lax.axis_index("outer") * 16 + lax.axis_index("inner")
+    greet_all()
+
+    def choose(d):
+        return [pot[pl.ds(pos[d, u], 1), :] for u in range(16)]
+
+    def go(t, carry):
+        to = peer(t)
+        d = to[0] * 16 + to[1]
+        for u, row in enumerate(choose(d)):
+            buf[d, u : u + 1, :] = row
+        pltpu.make_async_remote_copy(
+            src_ref=buf.at[d], dst_ref=dst.at[me], send_sem=send, recv_sem=recv, device_id=to, device_id_type=MESH
+        ).start()
+        return carry
+
+    lax.fori_loop(1, DEVS, go, 0)
+    for u, row in enumerate(choose(me)):
+        dst[me, u : u + 1, :] = row
+    most = pl.ds(0, DEVS - 1)
+    whole = pltpu.make_async_remote_copy(
+        src_ref=buf.at[most], dst_ref=dst.at[most], send_sem=send, recv_sem=recv,
+        device_id=peer(1), device_id_type=MESH,
+    )
+    whole.wait_recv()
+    whole.wait_send()
+
+
+def rows_back(pos, pot):
+    dma = pltpu.SemaphoreType.DMA
+    shape = (DEVS, 16, RHS)
+    return pl.pallas_call(
+        back_kernel,
+        out_shape=jax.ShapeDtypeStruct(shape, F32),
+        in_specs=[sspec(), vspec()],
+        out_specs=vspec(),
+        scratch_shapes=[pltpu.VMEM(shape, F32), dma, dma],
+        compiler_params=pltpu.CompilerParams(vmem_limit_bytes=VMEM_LIMIT, collective_id=2, has_side_effects=True),
+    )(pos, pot).reshape(ROWS, RHS)
 
 
 def gather_kernel(idx_ref, src_ref, dst_ref):
@@ -476,40 +645,13 @@
     )(idx, src)
 
 
-def tables(near, far):
-    o, i = lax.axis_index("outer"), lax.axis_index("inner")
-    y, c, x, z = o // 2, o % 2, i // 4, i % 4
-    rows = lax.dynamic_slice_in_dim(near, o * 64, 64, 0)
-    entry = rows[:, 1:].reshape(16, 28)
-    src, leaf = (entry // 4) % 16, entry % 4
-    target = jnp.arange(28, dtype=I32) // 7
-    earlier = jnp.arange(28)[:, None] > jnp.arange(28)[None, :]
-    nth = jnp.sum(((src[:, :, None] == src[:, None, :]) & earlier[None]).astype(I32), axis=2)
-    mark = 16 + 4 * target[None, :] + leaf
-    place = src * 2 + nth
-    hit = place[:, :, None] == jnp.arange(32, dtype=I32)[None, None, :]
-    code = jnp.sum(jnp.where(hit, mark[:, :, None], 0), axis=1).reshape(512)
-    mine = lax.dynamic_slice_in_dim(src, i, 1, 0)[0]
-    mine_nth = lax.dynamic_slice_in_dim(nth, i, 1, 0)[0]
-    near_at = (((x - mine // 4) % 4) * 4 + (z - mine % 4) % 4) * 2 + mine_nth
-    f = lax.dynamic_slice_in_dim(far, (o * 16 + i) * 4, 4, 0).reshape(32)
-    fo = f // 64
-    far_at = (((y - fo // 2) % 4) * 2 + (c + fo) % 2 - 1) * 4 + f % 4
-    return code.astype(I32), near_at.astype(I32), far_at.astype(I32)
-
-
 def shards(points, charges, interp, order, near, far, skel):
-    axes = ("outer", "inner")
-    code, near_at, far_at = tables(near, far)
-    rank, slot = (v.reshape(ROWS) for v in rank_rows(order))
-    sent = pack_rows(slot, order, points, charges).reshape(DEVS, 32, 128)
-    got = lax.all_to_all(sent, axes, split_axis=0, concat_axis=0, tiled=True)
-    pos = got[:, 16:32, DIM].astype(I32).reshape(ROWS)
-    blk, fblk, tgt, stgt = place_rows(pos, skel, got, interp)
-    pot = exchange(code, near_at, far_at, blk, fblk, tgt, stgt, interp)
-    back = gather_rows(pos, pot).reshape(DEVS, 16, RHS)
-    back = lax.all_to_all(back, axes, split_axis=0, concat_axis=0, tiled=True)
-    return gather_rows(rank, back.reshape(ROWS, RHS))
+    rank, slot, posmat, code, near_at, far_at = make_plan(order, near, far)
+    rank, slot = rank.reshape(ROWS), slot.reshape(ROWS)
+    got, pos = rows_out(pack_rows(rank, slot, points, charges, posmat))
+    blk, pts = place_rows(pos, got)
+    pot = exchange(code, near_at, far_at, skel, blk, pts, interp)
+    return gather_rows(rank, rows_back(pos, pot))
 
 
 def solution(mesh):

time: 204 us -> 189 us (0.926)
  Pallas kernels: 135 us -> 189 us
  waiting for transfers between devices: 25.3 us -> 0 us
  blocking collectives: 24.4 us -> 0 us
  starting transfers between devices: 11.5 us -> 0 us
  other arithmetic: 4.59 us -> 0 us
  local copies, waits for them, and re-layouts: 2.89 us -> 0 us
    pallas_call x2 -> x4, Pallas kernels: 14.4 us -> 71.9 us  [the longest x1 36 us: rows_out(): pl.pallas_call(out_kernel, out_shape=[jax.ShapeDtypeStruct((DEVS, 32, 128...]
    all_to_all x1 -> x0, waiting for transfers between devices: 25.3 us -> none  [shards(): got = lax.all_to_all(sent, axes, split_axis=0, concat_axis=0, tiled=True)]
    all_to_all x1 -> x0, blocking collectives: 24.4 us -> none  [shards(): back = lax.all_to_all(back, axes, split_axis=0, concat_axis=0, tiled=True)]
    all_to_all x1 -> x0, starting transfers between devices: 11.5 us -> none  [shards(): got = lax.all_to_all(sent, axes, split_axis=0, concat_axis=0, tiled=True)]
    pallas_call x2 -> x1, Pallas kernels: 8.85 us -> 4.43 us  [gather_rows(): pl.pallas_call(gather_kernel, out_shape=jax.ShapeDtypeStruct((ROWS, RHS),...]
    convert_element_type x1 -> x0, other arithmetic: 2.52 us -> none  [shards(): pos = got[:, 16:32, DIM].astype(I32).reshape(ROWS)]
  transfers between devices with their start and end apart: 1 -> 0, of which waited for: 1 -> 0; matrix products, arithmetic and copies ran while one was open for 2% -> 0% of each run, Pallas kernels for 0% -> 0%
where the time goes in v3:
time: 189 us
  Pallas kernels  189 us (100%)
    pallas_call x1, Pallas kernels, exchange(): pl.pallas_call(exchange_kernel, out_shape=jax.ShapeDtypeStruct((ROWS, RHS...  106 us
    pallas_call x1, Pallas kernels, rows_out(): pl.pallas_call(out_kernel, out_shape=[jax.ShapeDtypeStruct((DEVS, 32, 128...  36 us
    pallas_call x1, Pallas kernels, rows_back(): pl.pallas_call(back_kernel, out_shape=jax.ShapeDtypeStruct(shape, F32), i...  24.4 us
    pallas_call x1, Pallas kernels, place_rows(): pl.pallas_call(place_kernel, out_shape=[jax.ShapeDtypeStruct((8 * BLK, 12...  9.1 us
    pallas_call x1, Pallas kernels, pack_rows(): pl.pallas_call(send_kernel, out_shape=jax.ShapeDtypeStruct((DEVS * 32, 12...  6.47 us
    pallas_call x1, Pallas kernels, gather_rows(): pl.pallas_call(gather_kernel, out_shape=jax.ShapeDtypeStruct((ROWS, RHS),...  4.43 us

profile of v3, /device:TPU:1, one launch (start us, length us, event | category | flops | bytes accessed | tf_op | source)
XLA Modules:
  0.0 188.7 jit_solution(6041047058012375255)
XLA Ops:
  0.0 2.5 %shard_map.73 = (s32[16,128]{1,0:T(8,128)}, s32[16,128]{1,0:T(8,128)}, f32[128,128]{1,0:T(8,128)}, s32[32,512]{1,0:T(8,128)}, s32[8,512]{1,0:T(8,128)}, /*index=5*/s32[8,512]{1,0:T(8,128)}) custom-call(s32[16,128]{1,0:T(8,128)} %bitcast.20, s32[8,512]{1,0:T(8,128)} %bitcast.17, s32[8,512]{1,0:T(8,128)} %bitcast.18), custom_call_target="tpu_custom_call" | custom-call | tf_op jit(solution)/shard_map/pallas_call | solution.py:110
  2.5 6.5 %shard_map.74 = f32[4096,128]{1,0:T(8,128)} custom-call(s32[2048]{0:T(1024)} %bitcast.15, s32[2048]{0:T(1024)} %bitcast.19, f32[64,2048]{1,0:T(8,128)} %bitcast.14, f32[2048,128]{1,0:T(8,128)} %chg_ref.1, f32[128,128]{1,0:T(8,128)} %get-tuple-element.17.posmat_ref), custom_call_target="tpu_custom_call" | custom-call | tf_op jit(solution)/shard_map/pallas_call | solution.py:154
  9.0 36.0 %shard_map.75 = (f32[128,32,128]{2,1,0:T(8,128)}, s32[128,128]{1,0:T(8,128)}) custom-call(f32[128,32,128]{2,1,0:T(8,128)} %bitcast.10), custom_call_target="tpu_custom_call" | custom-call | tf_op jit(solution)/shard_map/pallas_call | solution.py:211
  44.9 9.1 %shard_map.76 = (f32[3072,128]{1,0:T(8,128)}, f32[2048,128]{1,0:T(8,128)}) custom-call(s32[128,128]{1,0:T(8,128)} %get-tuple-element.18.pos_ref.pos, f32[4096,128]{1,0:T(8,128)} %bitcast.12), custom_call_target="tpu_custom_call" | custom-call | tf_op jit(solution)/shard_map/pallas_call | solution.py:251
  54.0 105.8 %shard_map.77.pot = f32[2048,128]{1,0:T(8,128)} custom-call(s32[32,512]{1,0:T(8,128)} %get-tuple-element.19.code, s32[8,512]{1,0:T(8,128)} %get-tuple-element.20.near_at, s32[8,512]{1,0:T(8,128)} %get-tuple-element.21.far_at, s32[4,256]{1,0:T(4,128)} %skel.1, f32[2,4,384,128]{3,2,1,0:T(8,128)} %bitcast.13, f32[2048,128]{1,0:T(8,128)} %get-tuple-element.24.pts, ...), custom_call_target="tpu_custom_call" | custom-call | tf_op jit(solution)/shard_map/pallas_call | solution.py:553
  159.9 24.4 %shard_map.78 = f32[128,16,128]{2,1,0:T(8,128)} custom-call(s32[128,128]{1,0:T(8,128)} %get-tuple-element.18.pos_ref.pos, f32[2048,128]{1,0:T(8,128)} %shard_map.77.pot), custom_call_target="tpu_custom_call" | custom-call | tf_op jit(solution)/shard_map/pallas_call | solution.py:617
  184.3 4.4 %shard_map.79 = f32[2048,128]{1,0:T(8,128)} custom-call(s32[2048]{0:T(1024)} %bitcast.16, f32[2048,128]{1,0:T(8,128)} %bitcast.11), custom_call_target="tpu_custom_call" | custom-call | tf_op jit(solution)/shard_map/pallas_call | solution.py:639

commit v4 on v3

v4 whole, which is shorter than its diff:
```python
import functools
import math

import jax
import jax.numpy as jnp
from jax import lax
from jax.experimental import pallas as pl
from jax.experimental.pallas import tpu as pltpu
from jax.sharding import PartitionSpec as P

F32, BF16, I32 = jnp.float32, jnp.bfloat16, jnp.int32
MESH = pl.DeviceIdType.MESH
VMEM_LIMIT = 60 * 1024 * 1024

ROWS = 2048
DEVS = 128
LEAF = 512
HALF = 256
DIM = 64
RHS = 128
BLK = HALF + 128
SCALE = math.log2(math.e) * 4.0 / DIM


def vspec():
    return pl.BlockSpec(memory_space=pltpu.VMEM)


def sspec():
    return pl.BlockSpec(memory_space=pltpu.SMEM)


def dot(a, b, contract=((1,), (0,))):
    return lax.dot_general(a, b, (contract, ((), ())), preferred_element_type=F32)


def hi_lo(v):
    hi = v.astype(BF16)
    return hi, (v - hi.astype(F32)).astype(BF16)


def dot3(a, b, contract=((1,), (0,))):
    ah, al = hi_lo(a)
    bh, bl = hi_lo(b)
    return dot(ah, bh, contract) + dot(ah, bl, contract) + dot(al, bh, contract)


def three(v):
    hi = v.astype(BF16).astype(F32)
    rest = v - hi
    mid = rest.astype(BF16).astype(F32)
    return hi, mid, rest - mid


def plan_kernel(order_ref, near_ref, far_ref, sort_ref, posmat_ref, code_ref, near_at_ref, far_at_ref):
    sub = lax.broadcasted_iota(I32, (128, 128), 0)
    lane = lax.broadcasted_iota(I32, (128, 128), 1)
    before = (sub < lane).astype(F32).astype(BF16)
    ones = jnp.ones((128, 128), BF16)
    base = jnp.zeros((128, 128), F32)
    both = jnp.zeros((512, 16), F32)
    for r in range(ROWS // 128):
        order = order_ref[r : r + 1, :]
        owner = order >> 11
        hit = (sub == owner).astype(F32)
        hit16 = hit.astype(BF16)
        seen = dot(hit16, before) + base
        base = base + dot(hit16, ones)
        nth = jnp.sum(hit * seen, axis=0, keepdims=True).astype(I32)
        pos = ((order >> 8) & 1) * 1024 + ((order >> 9) & 3) * HALF + (order & 255)
        slot = (sub[0:16] == nth).astype(F32).astype(BF16)
        row = lane[0:1] + r * 128
        pieces = [(hit * v.astype(F32)).astype(BF16) for v in (pos >> 4, pos & 15, row >> 4, row & 15)]
        both = both + dot(jnp.concatenate(pieces, axis=0), slot, ((1,), (1,)))
    rest = jnp.zeros((128, 112), F32)
    posmat_ref[...] = jnp.concatenate([16.0 * both[0:128] + both[128:256], rest], axis=1)
    sort_ref[...] = jnp.concatenate([16.0 * both[256:384] + both[384:512], rest], axis=1).astype(I32)

    o, i = lax.axis_index("outer"), lax.axis_index("inner")
    y, c, x, z = o >> 1, o & 1, i >> 2, i & 3
    entry = near_ref[...]
    row = lax.broadcasted_iota(I32, entry.shape, 0)
    g = lax.broadcasted_iota(I32, entry.shape, 1) & 3
    src = jnp.where(row == 0, -1, (entry >> 2) & 15)
    nth = jnp.zeros(entry.shape, I32)
    for back in range(4):
        other = src if back == 0 else pltpu.roll(src, back, axis=1)
        for k in range(1, 8):
            earlier = (row > k) if back == 0 else (g >= back)
            nth = nth + jnp.where((other[k : k + 1, :] == src) & earlier, 1, 0)
    place = src * 2 + nth
    mark = 16 + 4 * g + (entry & 3)
    want = lax.broadcasted_iota(I32, (32, entry.shape[1]), 0)
    code = jnp.zeros(want.shape, I32)
    for k in range(1, 8):
        code = code + jnp.where(want == place[k : k + 1, :], mark[k : k + 1, :], 0)
    n = code.shape[1]
    code = code + pltpu.roll(code, n - 1, axis=1)
    code_ref[...] = code + pltpu.roll(code, n - 2, axis=1)
    near_at_ref[...] = ((((x - (src >> 2)) & 3) * 4 + ((z - src) & 3)) * 2 + nth) & 31
    f = far_ref[...]
    fo = f >> 6
    far_at_ref[...] = ((((y - (fo >> 1)) & 3) * 2 + ((c + fo) & 1)) - 1) * 4 + (f & 3)


def make_plan(order, near, far):
    leaves = near.shape[0]
    sd = jax.ShapeDtypeStruct
    return pl.pallas_call(
        plan_kernel,
        out_shape=[
            sd((DEVS, 128), I32),
            sd((DEVS, 128), F32),
            sd((32, leaves), I32),
            sd((8, leaves), I32),
            sd((8, leaves), I32),
        ],
        in_specs=[vspec()] * 3,
        out_specs=[vspec()] * 5,
    )(order.reshape(ROWS // 128, 128), near.T, far.T)


SENT = 25


def peer(t):
    o, i = lax.axis_index("outer"), lax.axis_index("inner")
    y, c, x, z = o >> 1, o & 1, i >> 2, i & 3
    a, b, e, other = t & 3, (t >> 2) & 3, (t >> 4) & 3, t >> 6
    return ((((y + a) & 3) << 1) | (c ^ other), (((x + a + b) & 3) << 2) | ((z + e + 3 * a) & 3))


def greet_all():
    def greet(t, carry):
        pl.semaphore_signal(pltpu.get_barrier_semaphore(), inc=1, device_id=peer(t), device_id_type=MESH)
        return carry

    lax.fori_loop(1, DEVS, greet, 0)


def out_kernel(sort, posmat, pts, chg, dst, pos, wide, buf, send, recv):
    me = lax.axis_index("outer") * 16 + lax.axis_index("inner")
    rows = pl.ds(0, SENT)
    greet_all()
    for r in range(ROWS // 128):
        x = pts[:, r * 128 : (r + 1) * 128]
        wide[r * 128 : (r + 1) * 128, :] = jnp.transpose(jnp.concatenate([x, x], axis=0))
    left = lax.broadcasted_iota(I32, (1, 128), 1) < DIM

    def fill(ref, d):
        at = [sort[d, u] for u in range(16)]
        c = [chg[pl.ds(n, 1), :] for n in at]
        p = [wide[pl.ds(n, 1), :] for n in at]
        for u in range(16):
            ref[d, u : u + 1, :] = c[u]
        for u in range(8):
            ref[d, 16 + u : 17 + u, :] = jnp.where(left, p[u], p[u + 8])
        ref[d, 24:25, :] = posmat[pl.ds(d, 1), :]

    fill(dst, me)
    pl.semaphore_wait(pltpu.get_barrier_semaphore(), DEVS - 1)

    def go(t, carry):
        to = peer(t)
        d = to[0] * 16 + to[1]
        fill(buf, d)
        pltpu.make_async_remote_copy(
            src_ref=buf.at[d, rows], dst_ref=dst.at[me, rows], send_sem=send, recv_sem=recv,
            device_id=to, device_id_type=MESH,
        ).start()
        return carry

    lax.fori_loop(1, DEVS, go, 0)
    most = pl.ds(0, DEVS - 1)
    whole = pltpu.make_async_remote_copy(
        src_ref=buf.at[most, rows], dst_ref=dst.at[most, rows], send_sem=send, recv_sem=recv,
        device_id=peer(1), device_id_type=MESH,
    )
    whole.wait_recv()
    pos[...] = dst[:, 24, :].astype(I32)
    whole.wait_send()


def rows_out(sort, posmat, points, charges):
    dma = pltpu.SemaphoreType.DMA
    return pl.pallas_call(
        out_kernel,
        out_shape=[jax.ShapeDtypeStruct((DEVS, 32, 128), F32), jax.ShapeDtypeStruct((DEVS, 128), I32)],
        in_specs=[sspec(), vspec(), vspec(), vspec()],
        out_specs=[vspec()] * 2,
        scratch_shapes=[pltpu.VMEM((ROWS, 128), F32), pltpu.VMEM((DEVS, 32, 128), F32), dma, dma],
        compiler_params=pltpu.CompilerParams(vmem_limit_bytes=VMEM_LIMIT, collective_id=1, has_side_effects=True),
    )(sort, posmat, points.T, charges)


def place_kernel(pos_ref, got_ref, blk_ref, pts_ref, turned):
    def turn(b, carry):
        for u in range(8):
            d = b * 8 + u
            rows = got_ref[pl.ds(pl.multiple_of(d * 32 + 16, 8), 8), :]
            turned[pl.ds(pl.multiple_of(d * 8, 8), 8), :] = pltpu.roll(rows, DIM, axis=1)
        return carry

    lax.fori_loop(0, DEVS // 8, turn, 0)

    def place(b, carry):
        at = [pos_ref[b, u] for u in range(16)]
        row = [a + ((a >> 8) << 7) for a in at]
        base = pl.multiple_of(b * 32, 32)
        half = pl.multiple_of(b * 8, 8)
        c = [got_ref[pl.ds(base + u, 1), :] for u in range(16)]
        p = [got_ref[pl.ds(base + 16 + u, 1), :] for u in range(8)] + [turned[pl.ds(half + u, 1), :] for u in range(8)]
        for u in range(16):
            blk_ref[pl.ds(row[u], 1), :] = c[u]
            pts_ref[pl.ds(at[u], 1), :] = p[u]
        return carry

    lax.fori_loop(0, DEVS, place, 0)
    for k in range(8):
        xt = jnp.transpose(pts_ref[k * HALF : (k + 1) * HALF, :])
        blk_ref[k * BLK + HALF : k * BLK + HALF + 64, :] = xt[0:64, 0:128]
        blk_ref[k * BLK + HALF + 64 : (k + 1) * BLK, :] = xt[0:64, 128:256]


def place_rows(pos, got):
    blk, pts = pl.pallas_call(
        place_kernel,
        out_shape=[jax.ShapeDtypeStruct((8 * BLK, 128), F32), jax.ShapeDtypeStruct((ROWS, 128), F32)],
        in_specs=[sspec(), vspec()],
        out_specs=[vspec()] * 2,
        scratch_shapes=[pltpu.VMEM((DEVS * 8, 128), F32)],
        compiler_params=pltpu.CompilerParams(vmem_limit_bytes=VMEM_LIMIT),
    )(pos, got.reshape(DEVS * 32, 128))
    return blk.reshape(2, 4, BLK, 128), pts


def target_operand(x):
    n = x.shape[0]
    hi, lo = hi_lo(x * (2.0 * SCALE))
    norm = jnp.sum(x * x, axis=1, keepdims=True) * (-SCALE)
    n0, n1, n2 = three(norm)
    lane = lax.broadcasted_iota(I32, (n, DIM), 1)
    tail = jnp.where(
        lane == 0, n0, jnp.where(lane == 1, n1, jnp.where(lane == 2, n2, jnp.where(lane < 6, 1.0, 0.0)))
    )
    return jnp.concatenate([hi, hi, lo, tail.astype(BF16)], axis=1)


def source_operand(block, scale):
    xt = jnp.concatenate([block[HALF : HALF + 64, :], block[HALF + 64 : BLK, :]], axis=1)
    hi, lo = hi_lo(xt)
    norm = jnp.sum(xt * xt, axis=0, keepdims=True) * (-SCALE)
    n0, n1, n2 = three(norm)
    row = lax.broadcasted_iota(I32, (16, HALF), 0)
    tail = jnp.where(
        row < 3, 1.0, jnp.where(row == 3, n0, jnp.where(row == 4, n1, jnp.where(row == 5, n2, 0.0)))
    )
    right = jnp.concatenate([hi, lo, hi, tail.astype(BF16), jnp.zeros((48, HALF), BF16)], axis=0)
    chg = block[0:HALF, :]
    if scale is not None:
        chg = chg * scale
    ch, cl = hi_lo(chg)
    return right, jnp.concatenate([ch, cl], axis=1)


def tile(target, operand):
    right, both = operand
    n = target.shape[0]
    g = jnp.exp2(dot(target, right))
    gh, gl = hi_lo(g)
    wide = dot(jnp.concatenate([gh, gl], axis=0), both)
    return wide[:n, 0:128] + (wide[:n, 128:256] + wide[n:, 0:128])


CHAIN = ((0, 0), (1, 0), (1, 1), (2, 1), (2, 2), (3, 2))
BESIDE = (
    ((3, 0), 0, (-1, 0)),
    ((0, 3), 0, (0, -1)),
    ((1, 3), 1, (0, -1)),
    ((0, 1), 2, (-1, 0)),
    ((2, 0), 3, (0, -1)),
    ((2, 3), 4, (0, 1)),
    ((1, 2), 4, (-1, 0)),
    ((0, 2), 5, (1, 0)),
    ((3, 3), 5, (0, 1)),
    ((3, 1), 5, (0, -1)),
)
SIGN = (1, -1)


def exchange_kernel(
    code, near_at, far_at, skel, blk, pts, interp, pot,
    fblk, tgt, stgt, sk, h01, h02, h03, h04, h05, h11, h12, h13, h14, h15, sb, rb, fb, ob,
    sc, rc, ss, rs, sf, rf,
):
    o, i = lax.axis_index("outer"), lax.axis_index("inner")
    y, c, x, z = o >> 1, o & 1, i >> 2, i & 3
    hub = ((blk.at[0], h01, h02, h03, h04, h05), (blk.at[1], h11, h12, h13, h14, h15))
    mine = (o * 16 + i) * 4

    def at_inner(dx, dz):
        return (((x + dx) & 3) << 2) | ((z + dz) & 3)

    def from_me(h, offset, sign=1):
        return at_inner(sign * SIGN[h] * offset[0], sign * SIGN[h] * offset[1])

    def along_y(d):
        return ((((y + d) & 3) << 1) | c, i)

    sibling = ((y << 1) | (1 - c), i)

    barrier = pltpu.get_barrier_semaphore()
    peers = [(o, at_inner(*d)) for d in ((1, 0), (-1, 0), (0, 1), (0, -1))] + [along_y(1), along_y(-1), sibling]
    for one in peers:
        pl.semaphore_signal(barrier, inc=1, device_id=one, device_id_type=MESH)
    pl.semaphore_wait(barrier, len(peers))

    def copy(src, dst, send, recv, to):
        return pltpu.make_async_remote_copy(
            src_ref=src, dst_ref=dst, send_sem=send, recv_sem=recv, device_id=to, device_id_type=MESH
        )

    def chain(h, k, leaf):
        (ax, az), (bx, bz) = CHAIN[k - 1], CHAIN[k]
        to = (o, from_me(h, (bx - ax, bz - az)))
        return copy(hub[h][k - 1].at[leaf], hub[h][k].at[leaf], sc.at[h, k - 1, leaf], rc.at[h, k - 1, leaf], to)

    def beside(h, n):
        return copy(sb.at[h, n], rb.at[h, n], ss.at[h, n], rs.at[h, n], (o, from_me(h, BESIDE[n][2])))

    def fbuf(dy, dc, lo=0, n=4):
        return fb.at[pl.ds((dy * 2 + dc - 1) * 4 + lo, n)]

    far_copies = {
        "up": copy(fblk, fbuf(1, 0), sf.at[0], rf.at[0], along_y(1)),
        "down": copy(fblk, fbuf(3, 0), sf.at[1], rf.at[1], along_y(-1)),
        "own": copy(fblk, fbuf(0, 1), sf.at[2], rf.at[2], sibling),
        "up2": copy(fbuf(1, 0, 0, 2), fbuf(2, 0, 0, 2), sf.at[3], rf.at[3], along_y(1)),
        "down2": copy(fbuf(3, 0, 2, 2), fbuf(2, 0, 2, 2), sf.at[4], rf.at[4], along_y(-1)),
        "side1": copy(fbuf(1, 0), fbuf(1, 1), sf.at[5], rf.at[5], sibling),
        "side3": copy(fbuf(3, 0), fbuf(3, 1), sf.at[6], rf.at[6], sibling),
        "side2": copy(fbuf(2, 0), fbuf(2, 1), sf.at[7], rf.at[7], sibling),
    }

    def wanted(dest, src, j):
        return code[src * 2 + j, (o * 16 + dest) * 4]

    def choose(n):
        offset, k, way = BESIDE[n]
        for h in range(2):
            src, dest = from_me(h, CHAIN[k], -1), from_me(h, way)
            for j in range(2):
                leaf = wanted(dest, src, j) & 3
                sb[h, n, j] = blk[h, leaf] if k == 0 else hub[h][k][leaf]
            beside(h, n).start()

    def serve(k, leaf):
        for h in range(2):
            chain(h, k, leaf).wait_recv()
            if k < 5:
                chain(h, k + 1, leaf).start()

    def add_tile(h, offset, j, load):
        src = from_me(h, offset, -1)
        v = wanted(i, src, j)
        at = (((SIGN[h] * offset[0]) % 4) * 4 + (SIGN[h] * offset[1]) % 4) * 2 + j
        ob[at] += tile(tgt[(v >> 2) & 3], source_operand(load(v & 3), (v >> 4).astype(F32)))

    def chain_tiles(k):
        for h in range(2):
            for j in range(2):
                add_tile(h, CHAIN[k], j, lambda leaf, h=h: hub[h][k][leaf])

    def beside_tiles(n):
        for h in range(2):
            beside(h, n).wait_recv()
            for j in range(2):
                add_tile(h, BESIDE[n][0], j, lambda leaf, h=h, j=j: rb[h, n, j])

    def halves(g):
        return [pl.ds(h * 1024 + g * HALF, HALF) for h in range(2)]

    def prepare(g):
        def pick(b, carry):
            at = [skel[g, b * 16 + u] for u in range(16)]
            rows = [pts[pl.ds((q >> 8) * 1024 + g * HALF + (q & 255), 1), :] for q in at]
            for u in range(16):
                sk[pl.ds(b * 16 + u, 1), :] = rows[u]
            return carry

        lax.fori_loop(0, 16, pick, 0)
        skt = jnp.transpose(sk[...])
        fblk[g, HALF : HALF + 64, :] = skt[0:64, 0:128]
        fblk[g, HALF + 64 : BLK, :] = skt[0:64, 128:256]
        stgt[g] = target_operand(sk[:, 0:DIM])
        charges = jnp.zeros((HALF, RHS), F32)
        for h, rows in enumerate(halves(g)):
            tgt[g, h * HALF : (h + 1) * HALF, :] = target_operand(pts[rows, 0:DIM])
            weights = interp[g * LEAF + h * HALF : g * LEAF + (h + 1) * HALF, :]
            charges = charges + dot3(weights, blk[h, g, 0:HALF, :], ((0,), (0,)))
        fblk[g, 0:HALF, :] = charges

    def own_tiles(g):
        near = tile(tgt[g], source_operand(blk[0, g], None)) + tile(tgt[g], source_operand(blk[1, g], None))
        for h, rows in enumerate(halves(g)):
            pot[rows, :] = near[h * HALF : (h + 1) * HALF, :]

    def far_leaf(g):
        def one(k, q):
            return q + tile(stgt[g], source_operand(fb[far_at[k, mine + g]], None))

        q = lax.fori_loop(0, 8, one, jnp.zeros((HALF, 128), F32))
        more = dot3(interp[g * LEAF : (g + 1) * LEAF, :], q)
        for h, rows in enumerate(halves(g)):
            pot[rows, :] += more[h * HALF : (h + 1) * HALF, :]

    def zero(t, carry):
        ob[t] = jnp.zeros((LEAF, 128), F32)
        return carry

    for leaf in range(4):
        for h in range(2):
            chain(h, 1, leaf).start()
    choose(1)
    prepare(0)
    serve(1, 0)
    prepare(1)
    prepare(2)
    serve(1, 1)
    serve(2, 0)
    prepare(3)
    for name in ("up", "down", "own"):
        far_copies[name].start()
    lax.fori_loop(0, 32, zero, 0)
    serve(1, 2)
    serve(2, 1)
    own_tiles(0)
    own_tiles(1)
    serve(1, 3)
    serve(2, 2)
    choose(2)
    own_tiles(2)
    serve(2, 3)
    serve(3, 0)
    choose(3)
    own_tiles(3)
    serve(3, 1)
    serve(4, 0)
    chain_tiles(1)
    serve(3, 2)
    serve(4, 1)
    for name, more in (("up", ("up2", "side1")), ("down", ("down2", "side3")), ("own", ())):
        far_copies[name].wait_recv()
        for m in more:
            far_copies[m].start()
    chain_tiles(2)
    serve(3, 3)
    serve(4, 2)
    choose(4)
    beside_tiles(1)
    serve(4, 3)
    choose(0)
    serve(5, 0)
    choose(5)
    choose(6)
    for name in ("up2", "down2"):
        far_copies[name].wait_recv()
    far_copies["side2"].start()
    chain_tiles(3)
    serve(5, 1)
    chain_tiles(4)
    serve(5, 2)
    beside_tiles(2)
    serve(5, 3)
    for n in (7, 8, 9):
        choose(n)
    for name in ("side1", "side3", "side2"):
        far_copies[name].wait_recv()
    for g in range(4):
        far_leaf(g)
    chain_tiles(5)
    for n in (0, 3, 4, 6, 5, 8, 7, 9):
        beside_tiles(n)

    for g in range(4):
        at = [near_at[k, mine + g] for k in range(1, 8)]
        for h, rows in enumerate(halves(g)):
            total = pot[rows, :]
            for k in range(7):
                total = total + ob[at[k], h * HALF : (h + 1) * HALF, :]
            pot[rows, :] = total

    for h in range(2):
        for k in range(1, 6):
            for leaf in range(4):
                chain(h, k, leaf).wait_send()
        for n in range(10):
            beside(h, n).wait_send()
    for one in far_copies.values():
        one.wait_send()


def exchange(code, near_at, far_at, skel, blk, pts, interp):
    dma = pltpu.SemaphoreType.DMA
    return pl.pallas_call(
        exchange_kernel,
        out_shape=jax.ShapeDtypeStruct((ROWS, RHS), F32),
        in_specs=[sspec()] * 4 + [vspec()] * 3,
        out_specs=vspec(),
        scratch_shapes=[
            pltpu.VMEM((4, BLK, 128), F32),
            pltpu.VMEM((4, LEAF, 256), BF16),
            pltpu.VMEM((4, HALF, 256), BF16),
            pltpu.VMEM((HALF, 128), F32),
        ]
        + [pltpu.VMEM((4, BLK, 128), F32)] * 10
        + [
            pltpu.VMEM((2, 10, 2, BLK, 128), F32),
            pltpu.VMEM((2, 10, 2, BLK, 128), F32),
            pltpu.VMEM((28, BLK, 128), F32),
            pltpu.VMEM((32, LEAF, 128), F32),
            dma((2, 5, 4)),
            dma((2, 5, 4)),
            dma((2, 10)),
            dma((2, 10)),
            dma((8,)),
            dma((8,)),
        ],
        compiler_params=pltpu.CompilerParams(
            vmem_limit_bytes=VMEM_LIMIT, collective_id=0, has_side_effects=True
        ),
    )(code, near_at, far_at, skel, blk, pts, interp)


def back_kernel(pos, pot, dst, buf, send, recv):
    me = lax.axis_index("outer") * 16 + lax.axis_index("inner")
    greet_all()
    pl.semaphore_wait(pltpu.get_barrier_semaphore(), DEVS - 1)

    def choose(d):
        return [pot[pl.ds(pos[d, u], 1), :] for u in range(16)]

    def go(t, carry):
        to = peer(t)
        d = to[0] * 16 + to[1]
        for u, row in enumerate(choose(d)):
            buf[d, u : u + 1, :] = row
        pltpu.make_async_remote_copy(
            src_ref=buf.at[d], dst_ref=dst.at[me], send_sem=send, recv_sem=recv, device_id=to, device_id_type=MESH
        ).start()
        return carry

    lax.fori_loop(1, DEVS, go, 0)
    for u, row in enumerate(choose(me)):
        dst[me, u : u + 1, :] = row
    most = pl.ds(0, DEVS - 1)
    whole = pltpu.make_async_remote_copy(
        src_ref=buf.at[most], dst_ref=dst.at[most], send_sem=send, recv_sem=recv,
        device_id=peer(1), device_id_type=MESH,
    )
    whole.wait_recv()
    whole.wait_send()


def rows_back(pos, pot):
    dma = pltpu.SemaphoreType.DMA
    shape = (DEVS, 16, RHS)
    return pl.pallas_call(
        back_kernel,
        out_shape=jax.ShapeDtypeStruct(shape, F32),
        in_specs=[sspec(), vspec()],
        out_specs=vspec(),
        scratch_shapes=[pltpu.VMEM(shape, F32), dma, dma],
        compiler_params=pltpu.CompilerParams(vmem_limit_bytes=VMEM_LIMIT, collective_id=2, has_side_effects=True),
    )(pos, pot).reshape(ROWS, RHS)


def spread_kernel(sort, src, dst):
    def body(b, carry):
        first = pl.multiple_of(b * 16, 16)
        to = [sort[b, u] for u in range(16)]
        rows = [src[pl.ds(first + u, 1), :] for u in range(16)]
        for u in range(16):
            dst[pl.ds(to[u], 1), :] = rows[u]
        return carry

    lax.fori_loop(0, DEVS, body, 0)


def spread_rows(sort, src):
    return pl.pallas_call(
        spread_kernel,
        out_shape=jax.ShapeDtypeStruct((ROWS, RHS), F32),
        in_specs=[sspec(), vspec()],
        out_specs=vspec(),
        compiler_params=pltpu.CompilerParams(vmem_limit_bytes=VMEM_LIMIT),
    )(sort, src)


def shards(points, charges, interp, order, near, far, skel):
    sort, posmat, code, near_at, far_at = make_plan(order, near, far)
    got, pos = rows_out(sort, posmat, points, charges)
    blk, pts = place_rows(pos, got)
    pot = exchange(code, near_at, far_at, skel, blk, pts, interp)
    return spread_rows(sort, rows_back(pos, pot))


def solution(mesh):
    rows = P(("outer", "inner"), None)
    return jax.shard_map(
        shards,
        mesh=mesh,
        in_specs=(rows, rows, rows, P(("outer", "inner")), P(), P(), rows),
        out_specs=rows,
        check_vma=False,
    )
```

time: 189 us -> 174 us (0.921)
  Pallas kernels: 189 us -> 174 us
    pallas_call x1, Pallas kernels: 106 us -> 95.5 us  [exchange(): pl.pallas_call(exchange_kernel, out_shape=jax.ShapeDtypeStruct((ROWS, RHS...]
    pallas_call x3 -> x2, Pallas kernels: 13.4 us -> 8.36 us  [the longest x1 4.99 us: spread_rows(): pl.pallas_call(spread_kernel, out_shape=jax.ShapeDtypeStruct((ROWS, RHS),...]
where the time goes in v4:
time: 174 us
  Pallas kernels  174 us (100%)
    pallas_call x1, Pallas kernels, exchange(): pl.pallas_call(exchange_kernel, out_shape=jax.ShapeDtypeStruct((ROWS, RHS...  95.5 us
    pallas_call x1, Pallas kernels, rows_out(): pl.pallas_call(out_kernel, out_shape=[jax.ShapeDtypeStruct((DEVS, 32, 128...  36.5 us
    pallas_call x1, Pallas kernels, rows_back(): pl.pallas_call(back_kernel, out_shape=jax.ShapeDtypeStruct(shape, F32), i...  24.1 us
    pallas_call x1, Pallas kernels, place_rows(): pl.pallas_call(place_kernel, out_shape=[jax.ShapeDtypeStruct((8 * BLK, 12...  9.08 us
    pallas_call x1, Pallas kernels, spread_rows(): pl.pallas_call(spread_kernel, out_shape=jax.ShapeDtypeStruct((ROWS, RHS),...  4.99 us

profile of v4, /device:TPU:1, one launch (start us, length us, event | category | flops | bytes accessed | tf_op | source)
XLA Modules:
  0.0 173.6 jit_solution(11426331990517843431)
XLA Ops:
  0.0 3.4 %shard_map.73 = (s32[128,128]{1,0:T(8,128)}, f32[128,128]{1,0:T(8,128)}, s32[32,512]{1,0:T(8,128)}, s32[8,512]{1,0:T(8,128)}, s32[8,512]{1,0:T(8,128)}) custom-call(s32[16,128]{1,0:T(8,128)} %bitcast.13, s32[8,512]{1,0:T(8,128)} %bitcast.11, s32[8,512]{1,0:T(8,128)} %bitcast.12), custom_call_target="tpu_custom_call" | custom-call | tf_op jit(solution)/shard_map/pallas_call | solution.py:109
  3.4 36.5 %shard_map.74 = (f32[128,32,128]{2,1,0:T(8,128)}, s32[128,128]{1,0:T(8,128)}) custom-call(s32[128,128]{1,0:T(8,128)} %get-tuple-element.14.sort, f32[128,128]{1,0:T(8,128)} %get-tuple-element.15.posmat, f32[64,2048]{1,0:T(8,128)} %bitcast.10, f32[2048,128]{1,0:T(8,128)} %chg.1), custom_call_target="tpu_custom_call" | custom-call | tf_op jit(solution)/shard_map/pallas_call | solution.py:186
  39.8 9.1 %shard_map.75 = (f32[3072,128]{1,0:T(8,128)}, f32[2048,128]{1,0:T(8,128)}) custom-call(s32[128,128]{1,0:T(8,128)} %get-tuple-element.16.pos_ref.pos, f32[4096,128]{1,0:T(8,128)} %bitcast.8), custom_call_target="tpu_custom_call" | custom-call | tf_op jit(solution)/shard_map/pallas_call | solution.py:226
  48.9 95.5 %shard_map.76.pot = f32[2048,128]{1,0:T(8,128)} custom-call(s32[32,512]{1,0:T(8,128)} %get-tuple-element.17.code, s32[8,512]{1,0:T(8,128)} %get-tuple-element.18.near_at, s32[8,512]{1,0:T(8,128)} %get-tuple-element.19.far_at, s32[4,256]{1,0:T(4,128)} %skel.1, f32[2,4,384,128]{3,2,1,0:T(8,128)} %bitcast.9, f32[2048,128]{1,0:T(8,128)} %get-tuple-element.22.pts, ...), custom_call_target="tpu_custom_call" | custom-call | tf_op jit(solution)/shard_map/pallas_call | solution.py:505
  144.4 24.1 %shard_map.77 = f32[128,16,128]{2,1,0:T(8,128)} custom-call(s32[128,128]{1,0:T(8,128)} %get-tuple-element.16.pos_ref.pos, f32[2048,128]{1,0:T(8,128)} %shard_map.76.pot), custom_call_target="tpu_custom_call" | custom-call | tf_op jit(solution)/shard_map/pallas_call | solution.py:568
  168.6 5.0 %shard_map.78 = f32[2048,128]{1,0:T(8,128)} custom-call(s32[128,128]{1,0:T(8,128)} %get-tuple-element.14.sort, f32[2048,128]{1,0:T(8,128)} %bitcast.7), custom_call_target="tpu_custom_call" | custom-call | tf_op jit(solution)/shard_map/pallas_call | solution.py:591

commit v5 on v4

--- a/solution.py
+++ b/solution.py
@@ -52,7 +52,15 @@
     return hi, mid, rest - mid
 
 
-def plan_kernel(order_ref, near_ref, far_ref, sort_ref, posmat_ref, code_ref, near_at_ref, far_at_ref):
+def widened(v):
+    return jnp.concatenate([v, jnp.zeros((128, 112), F32)], axis=1)
+
+
+def slots_first(v):
+    return jnp.transpose(widened(v))[0:16, :].astype(I32) & (ROWS - 1)
+
+
+def plan(order_ref, near_ref, far_ref, rank_ref, sort_ref, posmat_ref, code_ref, near_at_ref, far_at_ref):
     sub = lax.broadcasted_iota(I32, (128, 128), 0)
     lane = lax.broadcasted_iota(I32, (128, 128), 1)
     before = (sub < lane).astype(F32).astype(BF16)
@@ -67,14 +75,14 @@
         seen = dot(hit16, before) + base
         base = base + dot(hit16, ones)
         nth = jnp.sum(hit * seen, axis=0, keepdims=True).astype(I32)
+        rank_ref[r : r + 1, :] = (owner * 16 + nth) & (ROWS - 1)
         pos = ((order >> 8) & 1) * 1024 + ((order >> 9) & 3) * HALF + (order & 255)
         slot = (sub[0:16] == nth).astype(F32).astype(BF16)
         row = lane[0:1] + r * 128
         pieces = [(hit * v.astype(F32)).astype(BF16) for v in (pos >> 4, pos & 15, row >> 4, row & 15)]
         both = both + dot(jnp.concatenate(pieces, axis=0), slot, ((1,), (1,)))
-    rest = jnp.zeros((128, 112), F32)
-    posmat_ref[...] = jnp.concatenate([16.0 * both[0:128] + both[128:256], rest], axis=1)
-    sort_ref[...] = jnp.concatenate([16.0 * both[256:384] + both[384:512], rest], axis=1).astype(I32)
+    posmat_ref[...] = widened(16.0 * both[0:128] + both[128:256])
+    sort_ref[...] = slots_first(16.0 * both[256:384] + both[384:512])
 
     o, i = lax.axis_index("outer"), lax.axis_index("inner")
     y, c, x, z = o >> 1, o & 1, i >> 2, i & 3
@@ -100,24 +108,8 @@
     near_at_ref[...] = ((((x - (src >> 2)) & 3) * 4 + ((z - src) & 3)) * 2 + nth) & 31
     f = far_ref[...]
     fo = f >> 6
-    far_at_ref[...] = ((((y - (fo >> 1)) & 3) * 2 + ((c + fo) & 1)) - 1) * 4 + (f & 3)
-
-
-def make_plan(order, near, far):
-    leaves = near.shape[0]
-    sd = jax.ShapeDtypeStruct
-    return pl.pallas_call(
-        plan_kernel,
-        out_shape=[
-            sd((DEVS, 128), I32),
-            sd((DEVS, 128), F32),
-            sd((32, leaves), I32),
-            sd((8, leaves), I32),
-            sd((8, leaves), I32),
-        ],
-        in_specs=[vspec()] * 3,
-        out_specs=[vspec()] * 5,
-    )(order.reshape(ROWS // 128, 128), near.T, far.T)
+    device = jnp.maximum(((y - (fo >> 1)) & 3) * 2 + ((c + fo) & 1), 1)
+    far_at_ref[...] = (device - 1) * 4 + (f & 3)
 
 
 SENT = 25
@@ -136,102 +128,6 @@
         return carry
 
     lax.fori_loop(1, DEVS, greet, 0)
-
-
-def out_kernel(sort, posmat, pts, chg, dst, pos, wide, buf, send, recv):
-    me = lax.axis_index("outer") * 16 + lax.axis_index("inner")
-    rows = pl.ds(0, SENT)
-    greet_all()
-    for r in range(ROWS // 128):
-        x = pts[:, r * 128 : (r + 1) * 128]
-        wide[r * 128 : (r + 1) * 128, :] = jnp.transpose(jnp.concatenate([x, x], axis=0))
-    left = lax.broadcasted_iota(I32, (1, 128), 1) < DIM
-
-    def fill(ref, d):
-        at = [sort[d, u] for u in range(16)]
-        c = [chg[pl.ds(n, 1), :] for n in at]
-        p = [wide[pl.ds(n, 1), :] for n in at]
-        for u in range(16):
-            ref[d, u : u + 1, :] = c[u]
-        for u in range(8):
-            ref[d, 16 + u : 17 + u, :] = jnp.where(left, p[u], p[u + 8])
-        ref[d, 24:25, :] = posmat[pl.ds(d, 1), :]
-
-    fill(dst, me)
-    pl.semaphore_wait(pltpu.get_barrier_semaphore(), DEVS - 1)
-
-    def go(t, carry):
-        to = peer(t)
-        d = to[0] * 16 + to[1]
-        fill(buf, d)
-        pltpu.make_async_remote_copy(
-            src_ref=buf.at[d, rows], dst_ref=dst.at[me, rows], send_sem=send, recv_sem=recv,
-            device_id=to, device_id_type=MESH,
-        ).start()
-        return carry
-
-    lax.fori_loop(1, DEVS, go, 0)
-    most = pl.ds(0, DEVS - 1)
-    whole = pltpu.make_async_remote_copy(
-        src_ref=buf.at[most, rows], dst_ref=dst.at[most, rows], send_sem=send, recv_sem=recv,
-        device_id=peer(1), device_id_type=MESH,
-    )
-    whole.wait_recv()
-    pos[...] = dst[:, 24, :].astype(I32)
-    whole.wait_send()
-
-
-def rows_out(sort, posmat, points, charges):
-    dma = pltpu.SemaphoreType.DMA
-    return pl.pallas_call(
-        out_kernel,
-        out_shape=[jax.ShapeDtypeStruct((DEVS, 32, 128), F32), jax.ShapeDtypeStruct((DEVS, 128), I32)],
-        in_specs=[sspec(), vspec(), vspec(), vspec()],
-        out_specs=[vspec()] * 2,
-        scratch_shapes=[pltpu.VMEM((ROWS, 128), F32), pltpu.VMEM((DEVS, 32, 128), F32), dma, dma],
-        compiler_params=pltpu.CompilerParams(vmem_limit_bytes=VMEM_LIMIT, collective_id=1, has_side_effects=True),
-    )(sort, posmat, points.T, charges)
-
-
-def place_kernel(pos_ref, got_ref, blk_ref, pts_ref, turned):
-    def turn(b, carry):
-        for u in range(8):
-            d = b * 8 + u
-            rows = got_ref[pl.ds(pl.multiple_of(d * 32 + 16, 8), 8), :]
-            turned[pl.ds(pl.multiple_of(d * 8, 8), 8), :] = pltpu.roll(rows, DIM, axis=1)
-        return carry
-
-    lax.fori_loop(0, DEVS // 8, turn, 0)
-
-    def place(b, carry):
-        at = [pos_ref[b, u] for u in range(16)]
-        row = [a + ((a >> 8) << 7) for a in at]
-        base = pl.multiple_of(b * 32, 32)
-        half = pl.multiple_of(b * 8, 8)
-        c = [got_ref[pl.ds(base + u, 1), :] for u in range(16)]
-        p = [got_ref[pl.ds(base + 16 + u, 1), :] for u in range(8)] + [turned[pl.ds(half + u, 1), :] for u in range(8)]
-        for u in range(16):
-            blk_ref[pl.ds(row[u], 1), :] = c[u]
-            pts_ref[pl.ds(at[u], 1), :] = p[u]
-        return carry
-
-    lax.fori_loop(0, DEVS, place, 0)
-    for k in range(8):
-        xt = jnp.transpose(pts_ref[k * HALF : (k + 1) * HALF, :])
-        blk_ref[k * BLK + HALF : k * BLK + HALF + 64, :] = xt[0:64, 0:128]
-        blk_ref[k * BLK + HALF + 64 : (k + 1) * BLK, :] = xt[0:64, 128:256]
-
-
-def place_rows(pos, got):
-    blk, pts = pl.pallas_call(
-        place_kernel,
-        out_shape=[jax.ShapeDtypeStruct((8 * BLK, 128), F32), jax.ShapeDtypeStruct((ROWS, 128), F32)],
-        in_specs=[sspec(), vspec()],
-        out_specs=[vspec()] * 2,
-        scratch_shapes=[pltpu.VMEM((DEVS * 8, 128), F32)],
-        compiler_params=pltpu.CompilerParams(vmem_limit_bytes=VMEM_LIMIT),
-    )(pos, got.reshape(DEVS * 32, 128))
-    return blk.reshape(2, 4, BLK, 128), pts
 
 
 def target_operand(x):
@@ -289,9 +185,10 @@
 
 
 def exchange_kernel(
-    code, near_at, far_at, skel, blk, pts, interp, pot,
-    fblk, tgt, stgt, sk, h01, h02, h03, h04, h05, h11, h12, h13, h14, h15, sb, rb, fb, ob,
-    sc, rc, ss, rs, sf, rf,
+    order, near, far, skel, pts_in, chg_in, interp, out,
+    rank_v, sort_v, posmat, code_v, near_v, far_v, pos_v, inv_v, rank, sort, code, near_at, far_at, pos, inv, st,
+    wide, packed, got, so, ro, blk, pts, pot, leaving, landed, fblk, tgt, stgt, sk, h01, h02, h03, h04, h05, h11, h12, h13, h14, h15, sb, rb, fb, ob,
+    sc, rc, ss, rs, sf, rf, sl, rl,
 ):
     o, i = lax.axis_index("outer"), lax.axis_index("inner")
     y, c, x, z = o >> 1, o & 1, i >> 2, i & 3
@@ -309,16 +206,97 @@
 
     sibling = ((y << 1) | (1 - c), i)
 
-    barrier = pltpu.get_barrier_semaphore()
-    peers = [(o, at_inner(*d)) for d in ((1, 0), (-1, 0), (0, 1), (0, -1))] + [along_y(1), along_y(-1), sibling]
-    for one in peers:
-        pl.semaphore_signal(barrier, inc=1, device_id=one, device_id_type=MESH)
-    pl.semaphore_wait(barrier, len(peers))
+    me = o * 16 + i
+    greet_all()
+    plan(order, near, far, rank_v, sort_v, posmat, code_v, near_v, far_v)
+
+    def to_scalars(k, src, dst):
+        return pltpu.make_async_copy(src, dst, st.at[k])
+
+    moves = [to_scalars(0, sort_v, sort), to_scalars(1, rank_v, rank), to_scalars(2, code_v, code)]
+    moves += [to_scalars(3, near_v, near_at), to_scalars(4, far_v, far_at)]
+    for one in moves:
+        one.start()
+    for r in range(ROWS // 128):
+        cols = pts_in[:, r * 128 : (r + 1) * 128]
+        wide[r * 128 : (r + 1) * 128, :] = jnp.transpose(jnp.concatenate([cols, cols], axis=0))
+    for one in moves:
+        one.wait()
+    left = lax.broadcasted_iota(I32, (1, 128), 1) < DIM
+
+    def pack(ref, d):
+        at = [sort[u, d] for u in range(16)]
+        c16 = [chg_in[pl.ds(n, 1), :] for n in at]
+        p16 = [wide[pl.ds(n, 1), :] for n in at]
+        for u in range(16):
+            ref[d, u : u + 1, :] = c16[u]
+        for u in range(8):
+            ref[d, 16 + u : 17 + u, :] = jnp.where(left, p16[u], p16[u + 8])
+        ref[d, 24:25, :] = posmat[pl.ds(d, 1), :]
+
+    pack(got, me)
+    pl.semaphore_wait(pltpu.get_barrier_semaphore(), DEVS - 1)
 
     def copy(src, dst, send, recv, to):
         return pltpu.make_async_remote_copy(
             src_ref=src, dst_ref=dst, send_sem=send, recv_sem=recv, device_id=to, device_id_type=MESH
         )
+
+    sent_rows = pl.ds(0, SENT)
+    most = pl.ds(0, DEVS - 1)
+
+    def send_out(t, carry):
+        to = peer(t)
+        d = to[0] * 16 + to[1]
+        pack(packed, d)
+        copy(packed.at[d, sent_rows], got.at[me, sent_rows], so, ro, to).start()
+        return carry
+
+    lax.fori_loop(1, DEVS, send_out, 0)
+    all_out = copy(packed.at[most, sent_rows], got.at[most, sent_rows], so, ro, peer(1))
+    all_out.wait_recv()
+
+    arrived = jnp.transpose(got[:, 24, :])[0:16, :].astype(I32) & (ROWS - 1)
+    pos_v[...] = arrived
+    sub = lax.broadcasted_iota(I32, (128, 128), 0)
+    lane = lax.broadcasted_iota(I32, (128, 128), 1).astype(F32)
+    both = jnp.zeros((256, 16), F32)
+    for u in range(16):
+        p = arrived[u : u + 1, :]
+        hit = (sub == (p >> 4)).astype(F32)
+        low = (sub[0:16] == (p & 15)).astype(F32).astype(BF16)
+        pieces = jnp.concatenate([(hit * lane).astype(BF16), (hit * float(u)).astype(BF16)], axis=0)
+        both = both + dot(pieces, low, ((1,), (1,)))
+    inv_v[...] = slots_first(16.0 * both[0:128] + both[128:256])
+    moves = [to_scalars(5, pos_v, pos), to_scalars(6, inv_v, inv)]
+    for one in moves:
+        one.start()
+
+    def unpack(d, carry):
+        rows = got[d, 16:24, :]
+        wide[pl.ds(pl.multiple_of(d * 16, 16), 8), :] = rows
+        wide[pl.ds(pl.multiple_of(d * 16 + 8, 8), 8), :] = pltpu.roll(rows, DIM, axis=1)
+        return carry
+
+    lax.fori_loop(0, DEVS, unpack, 0)
+    for one in moves:
+        one.wait()
+
+    def place(h, g):
+        def some(b, carry):
+            at = [inv[u, h * 64 + g * 16 + b] for u in range(16)]
+            c16 = [got[n >> 4, pl.ds(n & 15, 1), :] for n in at]
+            p16 = [wide[pl.ds(n, 1), :] for n in at]
+            first = pl.multiple_of(b * 16, 16)
+            for u in range(16):
+                blk[h, g, pl.ds(first + u, 1), :] = c16[u]
+                pts[pl.ds(h * 1024 + g * HALF + first + u, 1), :] = p16[u]
+            return carry
+
+        lax.fori_loop(0, 16, some, 0)
+        xt = jnp.transpose(pts[h * 1024 + g * HALF : h * 1024 + (g + 1) * HALF, :])
+        blk[h, g, HALF : HALF + 64, :] = xt[0:64, 0:128]
+        blk[h, g, HALF + 64 : BLK, :] = xt[0:64, 128:256]
 
     def chain(h, k, leaf):
         (ax, az), (bx, bz) = CHAIN[k - 1], CHAIN[k]
@@ -420,6 +398,7 @@
 
     for leaf in range(4):
         for h in range(2):
+            place(h, leaf)
             chain(h, 1, leaf).start()
     choose(1)
     prepare(0)
@@ -490,6 +469,20 @@
                 total = total + ob[at[k], h * HALF : (h + 1) * HALF, :]
             pot[rows, :] = total
 
+    def gather(ref, at, d):
+        rows = [pot[pl.ds(pos[u, d], 1), :] for u in range(16)]
+        for u in range(16):
+            ref[at, u : u + 1, :] = rows[u]
+
+    def send_back(t, carry):
+        to = peer(t)
+        d = to[0] * 16 + to[1]
+        gather(leaving, d, d)
+        copy(leaving.at[d], landed.at[me], sl, rl, to).start()
+        return carry
+
+    lax.fori_loop(1, DEVS, send_back, 0)
+    gather(landed, me, me)
     for h in range(2):
         for k in range(1, 6):
             for leaf in range(4):
@@ -498,16 +491,56 @@
             beside(h, n).wait_send()
     for one in far_copies.values():
         one.wait_send()
-
-
-def exchange(code, near_at, far_at, skel, blk, pts, interp):
+    whole = copy(leaving.at[most], landed.at[most], sl, rl, peer(1))
+    whole.wait_recv()
+
+    def spread(b, carry):
+        first = pl.multiple_of(b * 16, 16)
+        at = [rank[b >> 3, (b & 7) * 16 + u] for u in range(16)]
+        rows = [landed[n >> 4, pl.ds(n & 15, 1), :] for n in at]
+        for u in range(16):
+            out[pl.ds(first + u, 1), :] = rows[u]
+        return carry
+
+    lax.fori_loop(0, ROWS // 16, spread, 0)
+    whole.wait_send()
+    all_out.wait_send()
+
+
+def exchange(order, near, far, skel, points, charges, interp):
     dma = pltpu.SemaphoreType.DMA
     return pl.pallas_call(
         exchange_kernel,
         out_shape=jax.ShapeDtypeStruct((ROWS, RHS), F32),
-        in_specs=[sspec()] * 4 + [vspec()] * 3,
+        in_specs=[vspec()] * 3 + [sspec()] + [vspec()] * 3,
         out_specs=vspec(),
         scratch_shapes=[
+            pltpu.VMEM((16, 128), I32),
+            pltpu.VMEM((16, 128), I32),
+            pltpu.VMEM((DEVS, 128), F32),
+            pltpu.VMEM((32, near.shape[0]), I32),
+            pltpu.VMEM((8, near.shape[0]), I32),
+            pltpu.VMEM((8, near.shape[0]), I32),
+            pltpu.VMEM((16, 128), I32),
+            pltpu.VMEM((16, 128), I32),
+            pltpu.SMEM((16, 128), I32),
+            pltpu.SMEM((16, 128), I32),
+            pltpu.SMEM((32, near.shape[0]), I32),
+            pltpu.SMEM((8, near.shape[0]), I32),
+            pltpu.SMEM((8, near.shape[0]), I32),
+            pltpu.SMEM((16, 128), I32),
+            pltpu.SMEM((16, 128), I32),
+            dma((7,)),
+            pltpu.VMEM((ROWS, 128), F32),
+            pltpu.VMEM((DEVS, 32, 128), F32),
+            pltpu.VMEM((DEVS, 32, 128), F32),
+            dma,
+            dma,
+            pltpu.VMEM((2, 4, BLK, 128), F32),
+            pltpu.VMEM((ROWS, 128), F32),
+            pltpu.VMEM((ROWS, RHS), F32),
+            pltpu.VMEM((DEVS, 16, RHS), F32),
+            pltpu.VMEM((DEVS, 16, RHS), F32),
             pltpu.VMEM((4, BLK, 128), F32),
             pltpu.VMEM((4, LEAF, 256), BF16),
             pltpu.VMEM((4, HALF, 256), BF16),
@@ -525,84 +558,17 @@
             dma((2, 10)),
             dma((8,)),
             dma((8,)),
+            dma,
+            dma,
         ],
         compiler_params=pltpu.CompilerParams(
             vmem_limit_bytes=VMEM_LIMIT, collective_id=0, has_side_effects=True
         ),
-    )(code, near_at, far_at, skel, blk, pts, interp)
-
-
-def back_kernel(pos, pot, dst, buf, send, recv):
-    me = lax.axis_index("outer") * 16 + lax.axis_index("inner")
-    greet_all()
-    pl.semaphore_wait(pltpu.get_barrier_semaphore(), DEVS - 1)
-
-    def choose(d):
-        return [pot[pl.ds(pos[d, u], 1), :] for u in range(16)]
-
-    def go(t, carry):
-        to = peer(t)
-        d = to[0] * 16 + to[1]
-        for u, row in enumerate(choose(d)):
-            buf[d, u : u + 1, :] = row
-        pltpu.make_async_remote_copy(
-            src_ref=buf.at[d], dst_ref=dst.at[me], send_sem=send, recv_sem=recv, device_id=to, device_id_type=MESH
-        ).start()
-        return carry
-
-    lax.fori_loop(1, DEVS, go, 0)
-    for u, row in enumerate(choose(me)):
-        dst[me, u : u + 1, :] = row
-    most = pl.ds(0, DEVS - 1)
-    whole = pltpu.make_async_remote_copy(
-        src_ref=buf.at[most], dst_ref=dst.at[most], send_sem=send, recv_sem=recv,
-        device_id=peer(1), device_id_type=MESH,
-    )
-    whole.wait_recv()
-    whole.wait_send()
-
-
-def rows_back(pos, pot):
-    dma = pltpu.SemaphoreType.DMA
-    shape = (DEVS, 16, RHS)
-    return pl.pallas_call(
-        back_kernel,
-        out_shape=jax.ShapeDtypeStruct(shape, F32),
-        in_specs=[sspec(), vspec()],
-        out_specs=vspec(),
-        scratch_shapes=[pltpu.VMEM(shape, F32), dma, dma],
-        compiler_params=pltpu.CompilerParams(vmem_limit_bytes=VMEM_LIMIT, collective_id=2, has_side_effects=True),
-    )(pos, pot).reshape(ROWS, RHS)
-
-
-def spread_kernel(sort, src, dst):
-    def body(b, carry):
-        first = pl.multiple_of(b * 16, 16)
-        to = [sort[b, u] for u in range(16)]
-        rows = [src[pl.ds(first + u, 1), :] for u in range(16)]
-        for u in range(16):
-            dst[pl.ds(to[u], 1), :] = rows[u]
-        return carry
-
-    lax.fori_loop(0, DEVS, body, 0)
-
-
-def spread_rows(sort, src):
-    return pl.pallas_call(
-        spread_kernel,
-        out_shape=jax.ShapeDtypeStruct((ROWS, RHS), F32),
-        in_specs=[sspec(), vspec()],
-        out_specs=vspec(),
-        compiler_params=pltpu.CompilerParams(vmem_limit_bytes=VMEM_LIMIT),
-    )(sort, src)
+    )(order.reshape(16, 128), near.T, far.T, skel, points.T, charges, interp)
 
 
 def shards(points, charges, interp, order, near, far, skel):
-    sort, posmat, code, near_at, far_at = make_plan(order, near, far)
-    got, pos = rows_out(sort, posmat, points, charges)
-    blk, pts = place_rows(pos, got)
-    pot = exchange(code, near_at, far_at, skel, blk, pts, interp)
-    return spread_rows(sort, rows_back(pos, pot))
+    return exchange(order, near, far, skel, points, charges, interp)
 
 
 def solution(mesh):

time: 174 us -> 166 us (0.954)
  Pallas kernels: 174 us -> 164 us
  local copies, waits for them, and re-layouts: 0 us -> 2.26 us
    pallas_call x5 -> x0, Pallas kernels: 78 us -> none  [the longest x1 36.5 us: rows_out(): pl.pallas_call(out_kernel, out_shape=[jax.ShapeDtypeStruct((DEVS, 32, 128...]
    pallas_call x1, Pallas kernels: 95.5 us -> 164 us  [exchange(): pl.pallas_call(exchange_kernel, out_shape=jax.ShapeDtypeStruct((ROWS, RHS...]
    unnamed x0 -> x1, local copies, waits for them, and re-layouts: none -> 2.26 us
where the time goes in v5:
time: 166 us
  Pallas kernels  164 us (99%)
  local copies, waits for them, and re-layouts  2.26 us (1%)
    pallas_call x1, Pallas kernels, exchange(): pl.pallas_call(exchange_kernel, out_shape=jax.ShapeDtypeStruct((ROWS, RHS...  164 us

profile of v5, /device:TPU:1, one launch (start us, length us, event | category | flops | bytes accessed | tf_op | source)
XLA Modules:
  0.0 166.1 jit_solution(2294933588754433107)
XLA Ops:
  0.0 163.8 %shard_map.73 = f32[2048,128]{1,0:T(8,128)} custom-call(s32[16,128]{1,0:T(8,128)} %bitcast.7, s32[8,512]{1,0:T(8,128)} %bitcast.5, s32[8,512]{1,0:T(8,128)} %bitcast.6, s32[4,256]{1,0:T(4,128)} %skel.1, f32[64,2048]{1,0:T(8,128)} %bitcast.4, f32[2048,128]{1,0:T(8,128)} %chg_in.1, f32[2048,256]{1,0:T(8,128)} %interp.1), custom_call_target="tpu_custom_call" | custom-call | tf_op jit(solution)/shard_map/pallas_call | solution.py:512
  163.8 2.3 %copy.9 = f32[2048,128]{1,0:T(8,128)} copy(f32[2048,128]{1,0:T(8,128)} %shard_map.73) | data formatting | bytes 2097152

commit v6 on v5

--- a/solution.py
+++ b/solution.py
@@ -185,7 +185,8 @@
 
 
 def exchange_kernel(
-    order, near, far, skel, pts_in, chg_in, interp, out,
+    order, near, far, skel, pts_hbm, chg_hbm, interp_hbm, out_hbm,
+    pts_in, chg_in, interp, out, sh,
     rank_v, sort_v, posmat, code_v, near_v, far_v, pos_v, inv_v, rank, sort, code, near_at, far_at, pos, inv, st,
     wide, packed, got, so, ro, blk, pts, pot, leaving, landed, fblk, tgt, stgt, sk, h01, h02, h03, h04, h05, h11, h12, h13, h14, h15, sb, rb, fb, ob,
     sc, rc, ss, rs, sf, rf, sl, rl,
@@ -207,6 +208,12 @@
     sibling = ((y << 1) | (1 - c), i)
 
     me = o * 16 + i
+    loads = [
+        pltpu.make_async_copy(src, dst, sh.at[k])
+        for k, (src, dst) in enumerate(((pts_hbm, pts_in), (chg_hbm, chg_in), (interp_hbm, interp)))
+    ]
+    for one in loads:
+        one.start()
     greet_all()
     plan(order, near, far, rank_v, sort_v, posmat, code_v, near_v, far_v)
 
@@ -217,6 +224,7 @@
     moves += [to_scalars(3, near_v, near_at), to_scalars(4, far_v, far_at)]
     for one in moves:
         one.start()
+    loads[0].wait()
     for r in range(ROWS // 128):
         cols = pts_in[:, r * 128 : (r + 1) * 128]
         wide[r * 128 : (r + 1) * 128, :] = jnp.transpose(jnp.concatenate([cols, cols], axis=0))
@@ -234,6 +242,7 @@
             ref[d, 16 + u : 17 + u, :] = jnp.where(left, p16[u], p16[u + 8])
         ref[d, 24:25, :] = posmat[pl.ds(d, 1), :]
 
+    loads[1].wait()
     pack(got, me)
     pl.semaphore_wait(pltpu.get_barrier_semaphore(), DEVS - 1)
 
@@ -245,15 +254,24 @@
     sent_rows = pl.ds(0, SENT)
     most = pl.ds(0, DEVS - 1)
 
-    def send_out(t, carry):
-        to = peer(t)
-        d = to[0] * 16 + to[1]
-        pack(packed, d)
-        copy(packed.at[d, sent_rows], got.at[me, sent_rows], so, ro, to).start()
+    def send_out(n, carry, count=2):
+        to = [peer(n * 2 - 1 + v) for v in range(count)]
+        d = [v[0] * 16 + v[1] for v in to]
+        for v in range(count):
+            pack(packed, d[v])
+        for v in range(count):
+            copy(packed.at[d[v], sent_rows], got.at[me, sent_rows], so, ro, to[v]).start()
         return carry
 
-    lax.fori_loop(1, DEVS, send_out, 0)
+    lax.fori_loop(1, DEVS // 2, send_out, 0)
+    send_out(DEVS // 2, 0, 1)
     all_out = copy(packed.at[most, sent_rows], got.at[most, sent_rows], so, ro, peer(1))
+
+    def zero(t, carry):
+        ob[t] = jnp.zeros((LEAF, 128), F32)
+        return carry
+
+    lax.fori_loop(0, 32, zero, 0)
     all_out.wait_recv()
 
     arrived = jnp.transpose(got[:, 24, :])[0:16, :].astype(I32) & (ROWS - 1)
@@ -392,15 +410,12 @@
         for h, rows in enumerate(halves(g)):
             pot[rows, :] += more[h * HALF : (h + 1) * HALF, :]
 
-    def zero(t, carry):
-        ob[t] = jnp.zeros((LEAF, 128), F32)
-        return carry
-
     for leaf in range(4):
         for h in range(2):
             place(h, leaf)
             chain(h, 1, leaf).start()
     choose(1)
+    loads[2].wait()
     prepare(0)
     serve(1, 0)
     prepare(1)
@@ -410,7 +425,6 @@
     prepare(3)
     for name in ("up", "down", "own"):
         far_copies[name].start()
-    lax.fori_loop(0, 32, zero, 0)
     serve(1, 2)
     serve(2, 1)
     own_tiles(0)
@@ -474,14 +488,17 @@
         for u in range(16):
             ref[at, u : u + 1, :] = rows[u]
 
-    def send_back(t, carry):
-        to = peer(t)
-        d = to[0] * 16 + to[1]
-        gather(leaving, d, d)
-        copy(leaving.at[d], landed.at[me], sl, rl, to).start()
+    def send_back(n, carry, count=2):
+        to = [peer(n * 2 - 1 + v) for v in range(count)]
+        d = [v[0] * 16 + v[1] for v in to]
+        for v in range(count):
+            gather(leaving, d[v], d[v])
+        for v in range(count):
+            copy(leaving.at[d[v]], landed.at[me], sl, rl, to[v]).start()
         return carry
 
-    lax.fori_loop(1, DEVS, send_back, 0)
+    lax.fori_loop(1, DEVS // 2, send_back, 0)
+    send_back(DEVS // 2, 0, 1)
     gather(landed, me, me)
     for h in range(2):
         for k in range(1, 6):
@@ -502,8 +519,15 @@
             out[pl.ds(first + u, 1), :] = rows[u]
         return carry
 
-    lax.fori_loop(0, ROWS // 16, spread, 0)
+    saves = []
+    for q in range(4):
+        lax.fori_loop(q * (ROWS // 64), (q + 1) * (ROWS // 64), spread, 0)
+        rows = pl.ds(q * (ROWS // 4), ROWS // 4)
+        saves.append(pltpu.make_async_copy(out.at[rows], out_hbm.at[rows], sh.at[3 + q]))
+        saves[-1].start()
     whole.wait_send()
+    for one in saves:
+        one.wait()
     all_out.wait_send()
 
 
@@ -512,9 +536,14 @@
     return pl.pallas_call(
         exchange_kernel,
         out_shape=jax.ShapeDtypeStruct((ROWS, RHS), F32),
-        in_specs=[vspec()] * 3 + [sspec()] + [vspec()] * 3,
-        out_specs=vspec(),
+        in_specs=[vspec()] * 3 + [sspec()] + [pl.BlockSpec(memory_space=pl.ANY)] * 3,
+        out_specs=pl.BlockSpec(memory_space=pl.ANY),
         scratch_shapes=[
+            pltpu.VMEM((DIM, ROWS), F32),
+            pltpu.VMEM((ROWS, RHS), F32),
+            pltpu.VMEM((ROWS, 256), F32),
+            pltpu.VMEM((ROWS, RHS), F32),
+            dma((7,)),
             pltpu.VMEM((16, 128), I32),
             pltpu.VMEM((16, 128), I32),
             pltpu.VMEM((DEVS, 128), F32),

time: 166 us -> 165 us (level)
  Pallas kernels: 164 us -> 162 us
    pallas_call x1, Pallas kernels: 164 us -> 162 us  [exchange(): pl.pallas_call(exchange_kernel, out_shape=jax.ShapeDtypeStruct((ROWS, RHS...]
where the time goes in v6:
time: 165 us; the launch traced here: 164 us
  Pallas kernels  162 us (98%)
  local copies, waits for them, and re-layouts  2.26 us (1%)
    pallas_call x1, Pallas kernels, exchange(): pl.pallas_call(exchange_kernel, out_shape=jax.ShapeDtypeStruct((ROWS, RHS...  162 us

profile of v6, /device:TPU:1, one launch (start us, length us, event | category | flops | bytes accessed | tf_op | source)
XLA Modules:
  0.0 164.4 jit_solution(7170704289975310199)
XLA Ops:
  0.0 162.1 %shard_map.73 = f32[2048,128]{1,0:T(8,128)} custom-call(s32[16,128]{1,0:T(8,128)} %bitcast.7, s32[8,512]{1,0:T(8,128)} %bitcast.5, s32[8,512]{1,0:T(8,128)} %bitcast.6, s32[4,256]{1,0:T(4,128)} %skel.1, f32[64,2048]{1,0:T(8,128)} %bitcast.4, f32[2048,128]{1,0:T(8,128)} %chg_hbm.1, f32[2048,256]{1,0:T(8,128)} %interp_hbm.1), custom_call_target="tpu_custom_call" | custom-call | tf_op jit(solution)/shard_map/pallas_call | solution.py:536
  162.1 2.3 %copy.9 = f32[2048,128]{1,0:T(8,128)} copy(f32[2048,128]{1,0:T(8,128)} %shard_map.73) | data formatting | bytes 2097152
